TPU v7x, 512 devices: a whole 4x4x16 slice. The times are simulated.
512 devices in a mesh: fsdp: 64 (over z, y), expert: 8 (over x, core).
Axes of the slice: x: 4, y: 4, z: 16, core: 2. Of those that a mesh axis runs over, the one named last changes fastest.
Arguments:
- grad: float32 [16, 3, 3584, 1024], P('expert', None, 'fsdp'), may hold values from -1000 to 1000
- momentum: float32 [16, 3, 3584, 1024], P('expert', None, 'fsdp'), may hold values from -120 to 120
- owners: int32 [16, 3], replicated, may hold values from 0 to 63, as said below
Outputs:
- momentum_new: float32 [16, 3, 3584, 1024], P('expert', None, 'fsdp')
- update: bfloat16 [16, 3, 3584, 1024], P('expert', None, 'fsdp')
- owned_rms: float32 [64], P('fsdp')
Inputs may be any that keep to these rules, and one draw needn't show every extreme that they name: `owners`: all 48 entries are different.
All inputs are finite; a program needn't handle non-finite values.
Results may differ from a plain program's by a relative error of at most 0.009.
Values may be sent and summed in bfloat16 or wider, within the bound.
No kernel may reach another device: no remote copies, remote signals or barrier semaphores. Data moves between devices by JAX's collectives and lax.ppermute only.
A program may use at most 64 MiB of HBM per device.

v0:
```python
import math

import jax
import jax.numpy as jnp
from jax import lax
from jax.sharding import PartitionSpec as P

D = 3584
FF = 1024
ITERS = 2


MU = 0.95
COEF_P = 3.4445
COEF_Q = -4.775
COEF_T = 2.0315


def newton_schulz(rows, owned):
    current = rows
    norm_sq = jnp.float32(0.0)
    for step in range(ITERS):
        partial_value = jnp.einsum(
            "rc,rd->cd", current, current, preferred_element_type=jnp.float32
        )
        gram = lax.psum(partial_value.astype(jnp.bfloat16), "expert").astype(jnp.float32)
        gram_half = gram.astype(jnp.bfloat16)
        if step == 0:
            norm_sq = jnp.trace(gram)
            scale = lax.rsqrt(jnp.where(owned, norm_sq, 1.0)) * owned.astype(jnp.float32)
            coef_p = COEF_P * scale
            coef_q = COEF_Q * scale * scale * scale
            coef_t = COEF_T * scale * scale * scale * scale * scale
        else:
            coef_p = jnp.float32(COEF_P)
            coef_q = jnp.float32(COEF_Q)
            coef_t = jnp.float32(COEF_T)
        if step == ITERS - 1:
            factor = jnp.float32(math.sqrt(D))
            coef_p = coef_p * factor
            coef_q = coef_q * factor
            coef_t = coef_t * factor
        product = jnp.dot(current, gram_half, preferred_element_type=jnp.float32)
        second = jnp.dot(
            product.astype(jnp.bfloat16), gram_half, preferred_element_type=jnp.float32
        )
        current = (
            coef_p * current.astype(jnp.float32) + coef_q * product + coef_t * second
        ).astype(jnp.bfloat16)
    return (current, norm_sq)


def shards(grad, momentum, owners):
    momentum_new = MU * momentum + grad
    blended = (grad + MU * momentum_new).astype(jnp.bfloat16)
    groups, kinds, shard_rows, width = blended.shape
    count = groups * kinds
    pieces = blended.reshape(count, shard_rows, width)
    n_fsdp = lax.axis_size("fsdp")
    n_expert = lax.axis_size("expert")
    subrows = shard_rows // n_expert
    flat_owner = owners.reshape(-1)
    slots = jnp.arange(n_fsdp, dtype=jnp.int32)
    table = (flat_owner[None, :] == slots[:, None]).astype(jnp.bfloat16)
    owned = jnp.sum(table.astype(jnp.float32), axis=1)[lax.axis_index("fsdp")] > 0.5
    own_table = lax.dynamic_slice_in_dim(table, lax.axis_index("expert") * count, count, 1)
    placed = jnp.einsum(
        "om,mrc->orc", own_table, pieces, preferred_element_type=jnp.float32
    ).astype(jnp.bfloat16)
    arrived = lax.all_to_all(placed, "fsdp", split_axis=0, concat_axis=0, tiled=True)
    split_rows = arrived.reshape(n_fsdp, n_expert, subrows, width)
    divided = lax.all_to_all(split_rows, "expert", split_axis=1, concat_axis=1, tiled=True)
    rows = (
        jnp.sum(divided.astype(jnp.float32), axis=1)
        .astype(jnp.bfloat16)
        .reshape(n_fsdp * subrows, width)
    )
    finished, norm_sq = newton_schulz(rows, owned)
    copies = jnp.broadcast_to(
        finished.reshape(n_fsdp, 1, subrows, width), (n_fsdp, n_expert, subrows, width)
    )
    gathered = lax.all_to_all(copies, "expert", split_axis=1, concat_axis=2, tiled=True)
    back = lax.all_to_all(
        gathered.reshape(n_fsdp, shard_rows, width), "fsdp", split_axis=0, concat_axis=0, tiled=True
    )
    update = jnp.einsum("om,orc->mrc", own_table, back, preferred_element_type=jnp.float32).astype(
        jnp.bfloat16
    )
    update = update.reshape(groups, kinds, shard_rows, width)
    owned_rms = jnp.sqrt(norm_sq / (D * FF)).reshape(1).astype(jnp.float32)
    return (momentum_new, update, owned_rms)


def solution(mesh):
    in_specs = (P("expert", None, "fsdp", None), P("expert", None, "fsdp", None), P())
    out_specs = (P("expert", None, "fsdp", None), P("expert", None, "fsdp", None), P("fsdp"))
    return jax.shard_map(shards, mesh=mesh, in_specs=in_specs, out_specs=out_specs, check_vma=False)
```

profile of v0, /device:TPU:1, one launch (start us, length us, event | category | flops | bytes accessed | tf_op | source)
XLA Modules:
  0.0 1083.8 jit_solution(2310193241454275121)
XLA Ops:
  7.2 0.0 all-reduce.3.cloned.1.call-start
  7.2 0.8 copy.24
  8.0 0.1 eq.19
  8.1 0.1 iota_compare_fusion.1
  8.1 3.3 add_convert_fusion.2
  11.4 2.1 convolution_convert_fusion
  13.6 7.1 copy.26
  20.7 340.3 %all_to_all.24 = bf16[64,56,1024]{2,1,0:T(8,128)(2,1)S(1)} all-to-all(bf16[64,56,1024]{2,1,0:T(8,128)(2,1)} %copy.26), channel_id=1, replica_groups=mesh['fsdp'=64,'expert'=8] {'fsdp'}, dimensions={0} | all-to-all | bytes 14680064 | tf_op jit(solution)/shard_map/all_to_all | solution.py:70
  361.0 7.1 copy.27
  368.1 94.1 %all_to_all.25 = bf16[64,8,7,1024]{3,0,2,1:T(8,128)(2,1)} all-to-all(bf16[64,8,7,1024]{3,0,2,1:T(8,128)(2,1)} %bitcast.23), channel_id=1, replica_groups=mesh['fsdp'=64,'expert'=8] {'expert'}, dimensions={1} | all-to-all | bytes 14680064 | tf_op jit(solution)/shard_map/all_to_all | solution.py:72
  462.2 5.0 reduce_sum.32
  467.1 2.6 bitcast_convert_fusion
  469.7 0.0 all-reduce.3.cloned.1.call-update
  469.7 0.3 all-reduce.5.cloned.1.call-start
  470.0 0.1 convert_reduce_fusion
  470.1 0.6 dynamic_slice.7
  471.3 0.5 copy.28
  471.9 0.3 reshape.35
  472.2 67.2 %all-reduce.3.cloned.1.call-done = bf16[1024,1024]{1,0:T(8,128)(2,1)} async-done(((bf16[1024,1024]{1,0:T(8,128)(2,1)}), bf16[1024,1024]{1,0:T(8,128)(2,1)}) %all-reduce.3.cloned.1.call-update) | async-done | bytes 2097168 | tf_op jit(solution)/shard_map/psum | solution.py:26
  539.4 0.0 copy-start
  539.4 2.5 select_reduce_fusion
  542.5 0.0 copy-done
  542.6 1.1 fusion.14
  543.7 1.2 add_convert_fusion.1
  544.9 0.0 copy-start.2
  544.9 0.9 copy-done.2
  545.8 2.6 convolution_convert_fusion.1
  548.4 0.0 copy-start.3
  548.4 0.0 all-reduce.5.cloned.1.call-update
  548.4 80.8 %all-reduce.5.cloned.1.call-done = bf16[1024,1024]{1,0:T(8,128)(2,1)} async-done(((bf16[1024,1024]{1,0:T(8,128)(2,1)}), bf16[1024,1024]{1,0:T(8,128)(2,1)}) %all-reduce.5.cloned.1.call-update) | async-done | bytes 2097168 | tf_op jit(solution)/shard_map/psum | solution.py:26
  629.2 0.0 copy-done.3
  629.3 0.0 copy-start.1
  629.3 2.9 fusion.15
  632.1 0.0 copy-done.1
  632.1 1.3 add_convert_fusion
  633.4 0.3 broadcast_in_dim.13
  633.7 0.6 copy.29
  634.3 0.9 broadcast_in_dim.14
  635.2 88.4 %all_to_all.26 = bf16[64,8,7,1024]{3,0,2,1:T(8,128)(2,1)S(1)} all-to-all(bf16[64,8,7,1024]{3,0,2,1:T(8,128)(2,1)S(1)} %broadcast_in_dim.14), channel_id=1, replica_groups=mesh['fsdp'=64,'expert'=8] {'expert'}, dimensions={1} | all-to-all | bytes 14680064 | tf_op jit(solution)/shard_map/all_to_all | solution.py:82
  723.6 7.1 copy.30
  730.8 15.8 %all-to-all-start.3 = ((bf16[64,56,1024]{2,1,0:T(8,128)(2,1)}), bf16[64,56,1024]{2,1,0:T(8,128)(2,1)}, u32[]{:S(2)}, u32[]{:S(2)}) async-start(bf16[64,56,1024]{2,1,0:T(8,128)(2,1)} %copy.30), calls=%async_computation.3 | async-start | bytes 14680064 | tf_op jit(solution)/shard_map/all_to_all | solution.py:83
  747.3 316.0 %all-to-all-done.3 = bf16[64,56,1024]{2,1,0:T(8,128)(2,1)} async-done(((bf16[64,56,1024]{2,1,0:T(8,128)(2,1)}), bf16[64,56,1024]{2,1,0:T(8,128)(2,1)}, u32[]{:S(2)}, u32[]{:S(2)}) %all-to-all-start.3) | async-done | bytes 7340064 | tf_op jit(solution)/shard_map/all_to_all | solution.py:83
  1063.3 10.8 fusion.2
  1074.2 1.2 copy.32
Async XLA Ops:
  7.2 532.2 %all-reduce.3.cloned.1.call-start = ((), (), s32[]{:S(2)}) async-start(), calls=%async_computation.4 | async-start | bytes 4194304 | tf_op jit(solution)/shard_map/psum | solution.py:26
  469.7 159.5 %all-reduce.5.cloned.1.call-start = ((), (), s32[]{:S(2)}) async-start(), calls=%async_computation.5 | async-start | bytes 4194304 | tf_op jit(solution)/shard_map/psum | solution.py:26
  539.4 3.2 copy-start
  544.9 0.9 copy-start.2
  548.4 80.8 %copy-start.3 = (bf16[448,1024]{1,0:T(8,128)(2,1)S(1)}, bf16[448,1024]{1,0:T(8,128)(2,1)}, u32[]{:S(2)}) copy-start(bf16[448,1024]{1,0:T(8,128)(2,1)} %copy-done.2) | copy-start | bytes 2752516
  629.3 2.9 copy-start.1
  730.8 332.5 %all-to-all-start.3 = ((bf16[64,56,1024]{2,1,0:T(8,128)(2,1)}), bf16[64,56,1024]{2,1,0:T(8,128)(2,1)}, u32[]{:S(2)}, u32[]{:S(2)}) async-start(bf16[64,56,1024]{2,1,0:T(8,128)(2,1)} %copy.30), calls=%async_computation.3 | async-start | bytes 14680064 | tf_op jit(solution)/shard_map/all_to_all | solution.py:83
Sparse Core Ops, SparseCore 0:
  469.9 69.4 all-reduce.2
  548.6 80.6 all-reduce.4
where the time goes:
time: 1100 us; the launch traced here: 1080 us
  blocking collectives  523 us (48%)
  waiting for transfers between devices  464 us (42%)
  local copies, waits for them, and re-layouts  27.5 us (2%)
  matrix products  24.6 us (2%)
  between operations  17.8 us (2%)
  starting transfers between devices  16.1 us (1%)
    all_to_all x1, blocking collectives, shards(): lax.all_to_all(placed, 'fsdp', split_axis=0, concat_axis=0, tiled=True)  340 us
    all_to_all x1, waiting for transfers between devices, shards(): lax.all_to_all(gathered.reshape(n_fsdp, shard_rows, width), 'fsdp', split...  316 us
    psum x2, waiting for transfers between devices, newton_schulz(): lax.psum(partial_value.astype(jnp.bfloat16), 'expert').astype(jnp.float32)  148 us
    all_to_all x1, blocking collectives, shards(): lax.all_to_all(split_rows, 'expert', split_axis=1, concat_axis=1, tiled=T...  94.1 us
    all_to_all x1, blocking collectives, shards(): lax.all_to_all(copies, 'expert', split_axis=1, concat_axis=2, tiled=True)  88.4 us
  transfers between devices with their start and end apart: 3, of which 3 were waited for; matrix products, arithmetic and copies ran while one was open for 0% of the time, Pallas kernels for 0%

commit v1 on v0

v1 whole, which is shorter than its diff:
```python
import math

import jax
import jax.numpy as jnp
from jax import lax
from jax.experimental import pallas as pl
from jax.experimental.pallas import tpu as pltpu
from jax.sharding import Mesh
from jax.sharding import PartitionSpec as P

D = 3584
FF = 1024
HALF = FF // 2
BLK = 256
SHARD = 56
ROWS = 64
CHUNK = 272
EXTRA = 16

MU = 0.95
COEF_P = 3.4445
COEF_Q = -4.775
COEF_T = 2.0315


F32 = jnp.float32
BF16 = jnp.bfloat16
VMEM = pl.BlockSpec(memory_space=pltpu.VMEM)
SMEM = pl.BlockSpec(memory_space=pltpu.SMEM)


def params(mib):
    return pltpu.CompilerParams(vmem_limit_bytes=mib * 1024 * 1024)


def dot(a, b):
    return jnp.dot(a, b, preferred_element_type=F32)


def dot_rows(a, b):
    return lax.dot_general(a, b, (((0,), (0,)), ((), ())), preferred_element_type=F32)


def blend_kernel(c_ref, grad_ref, mom_ref, new_ref, keep_ref, send_ref):
    first = c_ref[0] == 0
    grad = grad_ref[0]
    new = MU * mom_ref[0] + grad
    new_ref[0] = new
    blended = (grad + MU * new).astype(BF16)
    left, right = blended[:, :HALF], blended[:, HALF:]
    keep_ref[0] = jnp.where(first, left, right)
    send_ref[0] = jnp.where(first, right, left)


def blend(core, grad, momentum):
    count = grad.shape[0]
    full = pl.BlockSpec((1, SHARD, FF), lambda i: (i, 0, 0))
    half = pl.BlockSpec((1, SHARD, HALF), lambda i: (i, 0, 0))
    return pl.pallas_call(
        blend_kernel,
        grid=(count,),
        in_specs=[SMEM, full, full],
        out_specs=[full, half, half],
        out_shape=[
            jax.ShapeDtypeStruct((count, SHARD, FF), F32),
            jax.ShapeDtypeStruct((count, SHARD, HALF), BF16),
            jax.ShapeDtypeStruct((count, SHARD, HALF), BF16),
        ],
        compiler_params=params(16),
    )(core, grad, momentum)


def pack_kernel(c_ref, keep_ref, recv_ref, out_ref):
    c = c_ref[0]
    pad = jnp.zeros((ROWS - SHARD, HALF), F32)
    for k in range(4):
        for q in range(4):
            if k == 3:
                out_ref[k * 4 + q] = jnp.zeros((ROWS, HALF), BF16)
                continue
            i = (q % 2) * 3 + k
            piece = jnp.where(c == q // 2, keep_ref[i], recv_ref[i]).astype(F32)
            out_ref[k * 4 + q] = jnp.concatenate([piece, pad], axis=0).astype(BF16)


def pack(core, keep, recv):
    return pl.pallas_call(
        pack_kernel,
        in_specs=[SMEM, VMEM, VMEM],
        out_specs=VMEM,
        out_shape=jax.ShapeDtypeStruct((16, ROWS, HALF), BF16),
        compiler_params=params(16),
    )(core, keep, recv)


def index_grid(shape):
    return lax.broadcasted_iota(jnp.int32, shape, 0), lax.broadcasted_iota(jnp.int32, shape, 1)


def gram_kernel(c_ref, own_ref, oth_ref, out_ref, trace_ref):
    first = c_ref[0] == 0
    row, col = index_grid((BLK, BLK))
    x0, x1 = own_ref[:, :BLK], own_ref[:, BLK:]
    y0, y1 = oth_ref[:, :BLK], oth_ref[:, BLK:]
    g00, g11 = dot_rows(x0, x0), dot_rows(x1, x1)
    diag0 = jnp.sum(jnp.where(row == col, g00, 0.0), axis=0, keepdims=True)
    diag1 = jnp.sum(jnp.where(row == col, g11, 0.0), axis=0, keepdims=True)
    out_ref[0:BLK] = jnp.where(row <= col, g00, g11).astype(BF16)
    out_ref[BLK : 2 * BLK] = dot_rows(x0, x1).astype(BF16)
    out_ref[2 * BLK : 3 * BLK] = dot_rows(x0, jnp.where(first, y0, y1)).astype(BF16)
    out_ref[3 * BLK : 4 * BLK] = dot_rows(x1, jnp.where(first, y1, y0)).astype(BF16)
    out_ref[4 * BLK :] = jnp.broadcast_to(diag1, (4 * CHUNK - 4 * BLK, BLK)).astype(BF16)
    total = jnp.sum(diag0 + diag1, axis=1, keepdims=True)
    trace_ref[...] = jnp.broadcast_to(total, trace_ref.shape)


def partial_gram(core, own, oth):
    return pl.pallas_call(
        gram_kernel,
        in_specs=[SMEM, VMEM, VMEM],
        out_specs=[VMEM, VMEM],
        out_shape=[
            jax.ShapeDtypeStruct((4 * CHUNK, BLK), BF16),
            jax.ShapeDtypeStruct((16, 128), F32),
        ],
        compiler_params=params(32),
    )(core, own, oth)


def sum_kernel(parts_ref, t0_ref, t1_ref, t2_ref, t3_ref, out_ref):
    total = parts_ref[0].astype(F32) + parts_ref[1].astype(F32)
    total = total + (parts_ref[2].astype(F32) + parts_ref[3].astype(F32))
    out_ref[:CHUNK] = total.astype(BF16)
    row, _ = index_grid((EXTRA, 128))
    value = jnp.where(row < 4, t0_ref[...], t1_ref[...])
    value = jnp.where(row < 8, value, jnp.where(row < 12, t2_ref[...], t3_ref[...]))
    high = value.astype(BF16)
    out_ref[CHUNK:, :128] = high
    out_ref[CHUNK:, 128:] = (value - high.astype(F32)).astype(BF16)


def sum_parts(parts, traces):
    return pl.pallas_call(
        sum_kernel,
        in_specs=[VMEM] * 5,
        out_specs=VMEM,
        out_shape=jax.ShapeDtypeStruct((CHUNK + EXTRA, BLK), BF16),
        compiler_params=params(16),
    )(parts, *traces)


def unpack(ref):
    blocks, at = [], 0
    for _ in range(4):
        pieces, need = [], BLK
        while need:
            chunk, offset = divmod(at, CHUNK)
            take = min(need, CHUNK - offset)
            pieces.append(ref[chunk, offset : offset + take])
            at, need = at + take, need - take
        piece = pieces[0] if len(pieces) == 1 else jnp.concatenate(pieces, axis=0)
        blocks.append(piece.astype(F32))
    offset = at - 3 * CHUNK
    return blocks, ref[3, offset : offset + 16].astype(F32)[0:1]


def polynomial_kernel(
    c_ref, own_ref, oth_ref, xo_ref, xt_ref, out_ref, a32, ab, m32, mb, c32, cb, gb, w32, nb, wb
):
    first = c_ref[0] == 0
    row, col = index_grid((BLK, BLK))
    (d_o, o01, p2, p3), e_o = unpack(own_ref)
    (d_t, t01, r2, r3), e_t = unpack(oth_ref)

    extra = own_ref[0, CHUNK:].astype(F32) + oth_ref[0, CHUNK:].astype(F32)
    for i in range(1, 4):
        extra = extra + (own_ref[i, CHUNK:].astype(F32) + oth_ref[i, CHUNK:].astype(F32))
    norms = extra[:, :128] + extra[:, 128:]
    scale = lax.rsqrt(norms[0:1, 0:1])
    square = scale * scale

    def put(i, j, value):
        value = value * square
        a32[i * BLK : (i + 1) * BLK, j * BLK : (j + 1) * BLK] = value
        ab[i * BLK : (i + 1) * BLK, j * BLK : (j + 1) * BLK] = value.astype(BF16)

    def put_pair(i, j, value, turned):
        put(i, j, value)
        put(j, i, turned)

    for base, packed, edge, off in ((0, d_o, e_o, o01), (2, d_t, e_t, t01)):
        turned = packed.T
        put(base, base, jnp.where(row <= col, packed, turned))
        upper = jnp.where(row == col, jnp.broadcast_to(edge, (BLK, BLK)), turned)
        put(base + 1, base + 1, jnp.where(row > col, packed, upper))
        put_pair(base, base + 1, off, off.T)
    p2t, p3t, r2t, r3t = p2.T, p3.T, r2.T, r3.T
    put_pair(0, 2, jnp.where(first, p2, r2t), jnp.where(first, p2t, r2))
    put_pair(0, 3, jnp.where(first, r3t, p2), jnp.where(first, r3, p2t))
    put_pair(1, 2, jnp.where(first, r2t, p3), jnp.where(first, r2, p3t))
    put_pair(1, 3, jnp.where(first, p3, r3t), jnp.where(first, p3t, r3))

    blocks = [slice(i * BLK, (i + 1) * BLK) for i in range(4)]
    for s in blocks:
        poly = COEF_Q * a32[s] + COEF_T * dot(ab[s], ab[...])
        m32[s] = poly[:, :HALF]
        mb[s] = poly.astype(BF16)
    for s in blocks:
        prod = COEF_P * a32[s] + dot(ab[s], mb[...])
        c32[s] = prod
        cb[s] = prod.astype(BF16)
    for s in blocks:
        gram = COEF_P * c32[s] + dot(cb[s], mb[...])
        c32[s] = gram
        gb[s] = gram.astype(BF16)
    for s in blocks:
        poly = COEF_Q * c32[s, :HALF] + COEF_T * dot(gb[s], gb[:, :HALF])
        nb[s] = poly.astype(BF16)
        w32[s] = COEF_P * (poly + m32[s])
    for s in blocks:
        wb[s] = (w32[s] + dot(mb[s], nb[...])).astype(BF16)

    lanes = lax.broadcasted_iota(jnp.int32, (1, HALF), 1) // 128
    norm = jnp.where(lanes < 1, norms[0:1, 0:1], norms[4:5, 0:1])
    norm = jnp.where(lanes < 2, norm, jnp.where(lanes < 3, norms[8:9, 0:1], norms[12:13, 0:1]))
    high = norm.astype(BF16).astype(F32)
    spot = lax.broadcasted_iota(jnp.int32, (BLK, HALF), 0) % ROWS
    note = jnp.where(spot < ROWS - 4, high, norm - high)
    factor = scale * math.sqrt(D)
    for s in blocks:
        own = xo_ref[s]
        value = dot(own, wb[:HALF]) + dot(xt_ref[s], wb[HALF:])
        value = (value + (COEF_P * COEF_P) * own.astype(F32)) * factor
        out_ref[s] = jnp.where(spot < SHARD, value, note).astype(BF16)


def polynomial(core, own_gram, oth_gram, own, oth):
    square = (FF, FF)
    tall = (FF, HALF)
    return pl.pallas_call(
        polynomial_kernel,
        in_specs=[SMEM, VMEM, VMEM, VMEM, VMEM],
        out_specs=VMEM,
        out_shape=jax.ShapeDtypeStruct((16 * ROWS, HALF), BF16),
        scratch_shapes=[
            pltpu.VMEM(square, F32),
            pltpu.VMEM(square, BF16),
            pltpu.VMEM(tall, F32),
            pltpu.VMEM(square, BF16),
            pltpu.VMEM(square, F32),
            pltpu.VMEM(square, BF16),
            pltpu.VMEM(square, BF16),
            pltpu.VMEM(tall, F32),
            pltpu.VMEM(tall, BF16),
            pltpu.VMEM(tall, BF16),
        ],
        compiler_params=params(48),
    )(core, own_gram, oth_gram, own, oth)


def join_kernel(c_ref, own_ref, oth_ref, out_ref):
    first = c_ref[0] == 0
    own = own_ref[0].astype(F32)[:SHARD].astype(BF16)
    oth = oth_ref[0].astype(F32)[:SHARD].astype(BF16)
    out_ref[0, :, :HALF] = jnp.where(first, own, oth)
    out_ref[0, :, HALF:] = jnp.where(first, oth, own)


def join(core, own, oth):
    def slot(i, c):
        return ((i % 3) * 4 + 2 * c[0] + i // 3, 0, 0)

    return pl.pallas_call(
        join_kernel,
        grid_spec=pltpu.PrefetchScalarGridSpec(
            num_scalar_prefetch=1,
            grid=(6,),
            in_specs=[pl.BlockSpec((1, ROWS, HALF), slot)] * 2,
            out_specs=pl.BlockSpec((1, SHARD, FF), lambda i, c: (i, 0, 0)),
        ),
        out_shape=jax.ShapeDtypeStruct((6, SHARD, FF), BF16),
        compiler_params=params(16),
    )(core, own, oth)


def swap(value):
    return lax.ppermute(value, "c", [(0, 1), (1, 0)])


def owner_rms(notes, owners):
    spots = notes.reshape(3, 4, 8, 4, 128)[:, :, :, :, 0].astype(F32)
    norms = spots[:, :, 0] + spots[:, :, 4]
    x = lax.axis_index("x")
    table = owners.reshape(4, 4, 3)
    turned = jnp.stack([lax.dynamic_index_in_dim(table, (x - j) % 4, 0, False) for j in range(4)])
    me = (lax.axis_index("a") * 4 + lax.axis_index("b")) * 4 + lax.axis_index("y")
    mine = turned.transpose(2, 1, 0) == me
    return jnp.sqrt(jnp.sum(jnp.where(mine, norms, 0.0)) / (D * FF)).reshape(1)


def shards(grad, momentum, owners):
    shape = grad.shape
    core = lax.axis_index("c").astype(jnp.int32).reshape(1)
    flat = (6, SHARD, FF)
    momentum_new, keep, send = blend(core, grad.reshape(flat), momentum.reshape(flat))
    packed = pack(core, keep, swap(send))
    arrived = lax.all_to_all(packed, ("b", "y"), 0, 0, tiled=True)
    own = arrived.reshape(16 * ROWS, HALF)
    oth = swap(own)
    partial, trace = partial_gram(core, own, oth)
    traces = [trace] + [
        lax.ppermute(trace, "x", [(i, (i + j) % 4) for i in range(4)]) for j in (1, 2, 3)
    ]
    parts = lax.all_to_all(partial.reshape(4, CHUNK, BLK), "a", 0, 0, tiled=True)
    mine = sum_parts(parts, traces)
    own_gram = lax.all_gather(mine, "a", axis=0)
    oth_gram = swap(own_gram)
    finished = polynomial(core, own_gram, oth_gram, own, oth)
    back = lax.all_to_all(finished.reshape(16, ROWS, HALF), ("b", "y"), 0, 0, tiled=True)
    update = join(core, back, swap(back))
    owned_rms = owner_rms(back[:12, SHARD:], owners)
    return (momentum_new.reshape(shape), update.reshape(shape), owned_rms)


def solution(mesh):
    fine = Mesh(mesh.devices.reshape(4, 4, 4, 4, 2), ("a", "b", "y", "x", "c"))
    rows = ("a", "b", "y")
    wide = P(("x", "c"), None, rows, None)
    return jax.shard_map(
        shards, mesh=fine, in_specs=(wide, wide, P()), out_specs=(wide, wide, P(rows)), check_vma=False
    )
```

time: 1100 us -> 177 us (0.16); the launches traced: 1080 us -> 176 us
  waiting for transfers between devices: 464 us -> 14.2 us
  blocking collectives: 523 us -> 84.2 us
  starting transfers between devices: 16.1 us -> 54 us
  matrix products: 24.6 us -> 0 us
  local copies, waits for them, and re-layouts: 27.5 us -> 3.58 us
  Pallas kernels: 0 us -> 16.9 us
  between operations: 17.8 us -> 2.67 us
    all_to_all x3 -> x2, blocking collectives: 523 us -> 60.2 us  [the longest x1 32.5 us: shards(): lax.all_to_all(finished.reshape(16, ROWS, HALF), ('b', 'y'), 0, 0, tiled=...]
    all_to_all x1, waiting for transfers between devices: 316 us -> 7.44 us  [shards(): lax.all_to_all(partial.reshape(4, CHUNK, BLK), 'a', 0, 0, tiled=True)]
    psum x2 -> x0, waiting for transfers between devices: 148 us -> none  [newton_schulz(): lax.psum(partial_value.astype(jnp.bfloat16), 'expert').astype(jnp.float32)]
    ppermute x0 -> x7, starting transfers between devices: none -> 41.9 us  [the longest x4 31.4 us: swap(): return lax.ppermute(value, 'c', [(0, 1), (1, 0)])]
    dot_general x8 -> x0, matrix products: 24.6 us -> none  [the longest x1 10.8 us: shards(): jnp.einsum('om,orc->mrc', own_table, back, preferred_element_type=jnp.flo...]
    all_gather x0 -> x1, blocking collectives: none -> 24 us  [shards(): own_gram = lax.all_gather(mine, 'a', axis=0)]
    pallas_call x0 -> x6, Pallas kernels: none -> 16.9 us  [the longest x1 10.8 us: polynomial(): pl.pallas_call(polynomial_kernel, in_specs=[SMEM, VMEM, VMEM, VMEM, VMEM]...]
  transfers between devices with their start and end apart: 3 -> 8, of which waited for: 3 -> 5; matrix products, arithmetic and copies ran while one was open for 0% -> 1% of each run, Pallas kernels for 0% -> 0%
where the time goes in v1:
time: 177 us; the launch traced here: 176 us
  blocking collectives  84.2 us (48%)
  starting transfers between devices  54 us (31%)
  Pallas kernels  16.9 us (10%)
  waiting for transfers between devices  14.2 us (8%)
  local copies, waits for them, and re-layouts  3.58 us (2%)
  between operations  2.67 us (2%)
    all_to_all x1, blocking collectives, shards(): lax.all_to_all(finished.reshape(16, ROWS, HALF), ('b', 'y'), 0, 0, tiled=...  32.5 us
    ppermute x4, starting transfers between devices, swap(): return lax.ppermute(value, 'c', [(0, 1), (1, 0)])  31.4 us
    all_to_all x1, blocking collectives, shards(): arrived = lax.all_to_all(packed, ('b', 'y'), 0, 0, tiled=True)  27.7 us
    all_gather x1, blocking collectives, shards(): own_gram = lax.all_gather(mine, 'a', axis=0)  24 us
    all_to_all x1, starting transfers between devices, shards(): lax.all_to_all(partial.reshape(4, CHUNK, BLK), 'a', 0, 0, tiled=True)  12.1 us
    pallas_call x1, Pallas kernels, polynomial(): pl.pallas_call(polynomial_kernel, in_specs=[SMEM, VMEM, VMEM, VMEM, VMEM]...  10.8 us
    ppermute x3, starting transfers between devices, shards(): lax.ppermute(trace, 'x', [(i, (i + j) % 4) for i in range(4)])  10.5 us
    all_to_all x1, waiting for transfers between devices, shards(): lax.all_to_all(partial.reshape(4, CHUNK, BLK), 'a', 0, 0, tiled=True)  7.44 us
  transfers between devices with their start and end apart: 8, of which 5 were waited for; matrix products, arithmetic and copies ran while one was open for 1% of the time, Pallas kernels for 0%

profile of v1, /device:TPU:1, one launch (start us, length us, event | category | flops | bytes accessed | tf_op | source)
XLA Modules:
  0.0 176.2 jit_solution(6739874579117809659)
XLA Ops:
  0.6 0.0 copy-start
  0.6 1.3 copy-done
  2.0 0.0 copy-start.1
  2.0 1.3 copy-done.1
  3.3 2.3 %shard_map.58 = (f32[6,56,1024]{2,1,0:T(8,128)}, bf16[6,56,512]{2,1,0:T(8,128)(2,1)S(1)}, bf16[6,56,512]{2,1,0:T(8,128)(2,1)S(1)}) custom-call(s32[1]{0:T(128)} %bitcast.c_ref, f32[6,56,1024]{2,1,0:T(8,128)S(1)} %bitcast.27, f32[6,56,1024]{2,1,0:T(8,128)S(1)} %bitcast.28), custom_call_target="tpu_custom_call" | custom-call | tf_op jit(solution)/shard_map/pallas_call | solution.py:59
  5.6 8.8 %collective-permute-start = (bf16[6,56,512]{2,1,0:T(8,128)(2,1)S(1)}, bf16[6,56,512]{2,1,0:T(8,128)(2,1)S(1)}, u32[]{:S(2)}, u32[]{:S(2)}) collective-permute-start(bf16[6,56,512]{2,1,0:T(8,128)(2,1)S(1)} %get-tuple-element.10), channel_id=1, source_target_pairs={{0,1},{1,0},{2,3},{3,2},{4,5},{5,4},{6,7},{7,6},{8,9},{9,8},{10,11... | collective-permute-start | bytes 1032200 | tf_op jit(solution)/shard_map/ppermute | solution.py:287
  14.3 1.3 collective-permute-done.recv_ref
  15.6 0.1 shard_map.59
  15.7 27.7 %all_to_all.15 = bf16[16,64,512]{2,1,0:T(8,128)(2,1)S(1)} all-to-all(bf16[16,64,512]{2,1,0:T(8,128)(2,1)S(1)} %shard_map.59), channel_id=1, replica_groups=mesh['a'=4,'b'=4,'y'=4,'x'=4,'c'=2] {'b','y'}, dimensions={0} | all-to-all | bytes 2097152 | tf_op jit(solution)/shard_map/all_to_all | solution.py:307
  43.3 4.6 %collective-permute-start.1 = (bf16[1024,512]{1,0:T(8,128)(2,1)S(1)}, bf16[1024,512]{1,0:T(8,128)(2,1)S(1)}, u32[]{:S(2)}, u32[]{:S(2)}) collective-permute-start(bf16[1024,512]{1,0:T(8,128)(2,1)S(1)} %bitcast.21), channel_id=1, source_target_pairs={{0,1},{1,0},{2,3},{3,2},{4,5},{5,4},{6,7},{7,6},{8,9},{9,8},{10,11... | collective-permute-start | bytes 3145736 | tf_op jit(solution)/shard_map/ppermute | solution.py:287
  48.0 2.3 %collective-permute-done.1.oth_ref.xt_ref = bf16[1024,512]{1,0:T(8,128)(2,1)S(1)} collective-permute-done((bf16[1024,512]{1,0:T(8,128)(2,1)S(1)}, bf16[1024,512]{1,0:T(8,128)(2,1)S(1)}, u32[]{:S(2)}, u32[]{:S(2)}) %collective-permute-start.1) | collective-permute-done | bytes 1048608 | tf_op jit(solution)/shard_map/ppermute | solution.py:287
  50.2 1.7 shard_map.60
  51.9 12.1 %all-to-all-start.1 = ((bf16[4,272,256]{2,1,0:T(8,128)(2,1)}), bf16[4,272,256]{2,1,0:T(8,128)(2,1)S(1)}, u32[]{:S(2)}, u32[]{:S(2)}) async-start(bf16[4,272,256]{2,1,0:T(8,128)(2,1)} %bitcast.5), calls=%async_computation.1 | async-start | bytes 1114112 | tf_op jit(solution)/shard_map/all_to_all | solution.py:314
  64.0 3.1 %collective-permute-start.2 = (f32[16,128]{1,0:T(8,128)S(1)}, f32[16,128]{1,0:T(8,128)S(1)}, u32[]{:S(2)}, u32[]{:S(2)}) collective-permute-start(f32[16,128]{1,0:T(8,128)S(1)} %get-tuple-element.12.t0_ref), channel_id=1, source_target_pairs={{0,2},{2,4},{4,6},{6,0},{1,3},{3,5},{5,7},{7,1},{8,10},{10,12},{12... | collective-permute-start | bytes 24584 | tf_op jit(solution)/shard_map/ppermute | solution.py:312
  67.1 4.4 %collective-permute-start.3 = (f32[16,128]{1,0:T(8,128)S(1)}, f32[16,128]{1,0:T(8,128)S(1)}, u32[]{:S(2)}, u32[]{:S(2)}) collective-permute-start(f32[16,128]{1,0:T(8,128)S(1)} %get-tuple-element.12.t0_ref), channel_id=1, source_target_pairs={{0,4},{2,6},{4,0},{6,2},{1,5},{3,7},{5,1},{7,3},{8,12},{10,14},{12... | collective-permute-start | bytes 24584 | tf_op jit(solution)/shard_map/ppermute | solution.py:312
  71.5 3.1 %collective-permute-start.4 = (f32[16,128]{1,0:T(8,128)S(1)}, f32[16,128]{1,0:T(8,128)S(1)}, u32[]{:S(2)}, u32[]{:S(2)}) collective-permute-start(f32[16,128]{1,0:T(8,128)S(1)} %get-tuple-element.12.t0_ref), channel_id=1, source_target_pairs={{0,6},{2,0},{4,2},{6,4},{1,7},{3,1},{5,3},{7,5},{8,14},{10,8},{12,... | collective-permute-start | bytes 24584 | tf_op jit(solution)/shard_map/ppermute | solution.py:312
  74.6 0.0 collective-permute-done.2.t1_ref
  74.6 0.0 collective-permute-done.3.t2_ref
  74.6 1.6 collective-permute-done.4.t3_ref
  76.2 7.4 %all-to-all-done.1.parts_ref = bf16[4,272,256]{2,1,0:T(8,128)(2,1)S(1)} async-done(((bf16[4,272,256]{2,1,0:T(8,128)(2,1)}), bf16[4,272,256]{2,1,0:T(8,128)(2,1)S(1)}, u32[]{:S(2)}, u32[]{:S(2)}) %all-to-all-start.1) | async-done | bytes 557088 | tf_op jit(solution)/shard_map/all_to_all | solution.py:314
  83.6 0.1 shard_map.61
  83.7 24.0 %all-gather = bf16[1152,256]{1,0:T(8,128)(2,1)S(1)} all-gather(bf16[288,256]{1,0:T(8,128)(2,1)S(1)} %shard_map.61), channel_id=2, replica_groups=mesh['a'=4,'b'=4,'y'=4,'x'=4,'c'=2] {'a'}, dimensions={0}, use_global_device_ids=true | all-gather | bytes 737280 | tf_op jit(solution)/shard_map/all_gather | solution.py:316
  107.7 13.4 %collective-permute-start.5 = (bf16[4,288,256]{2,1,0:T(8,128)(2,1)S(1)}, bf16[4,288,256]{2,1,0:T(8,128)(2,1)S(1)}, u32[]{:S(2)}, u32[]{:S(2)}) collective-permute-start(bf16[4,288,256]{2,1,0:T(8,128)(2,1)S(1)} %bitcast.25), channel_id=1, source_target_pairs={{0,1},{1,0},{2,3},{3,2},{4,5},{5,4},{6,7},{7,6},{8,9},{9,8},{10,11... | collective-permute-start | bytes 1769480 | tf_op jit(solution)/shard_map/ppermute | solution.py:287
  121.1 1.6 collective-permute-done.5.oth_ref
  122.7 10.8 %shard_map.62 = bf16[1024,512]{1,0:T(8,128)(2,1)S(1)} custom-call(s32[1]{0:T(128)} %bitcast.c_ref, bf16[4,288,256]{2,1,0:T(8,128)(2,1)S(1)} %bitcast.26, bf16[4,288,256]{2,1,0:T(8,128)(2,1)S(1)} %collective-permute-done.5.oth_ref, bf16[1024,512]{1,0:T(8,128)(2,1)S(1)} %bitcast.23, bf16[1024,512]{1,0:T(8,128)(2,1)S(1)} %collective-permute-done.1.oth_ref.xt_ref), custom_call_target="tpu_custom_call" | custom-call | tf_op jit(solution)/shard_map/pallas_call | solution.py:240
  133.5 0.0 copy-start.2
  133.5 32.5 %all_to_all.16.own_ref = bf16[16,64,512]{2,1,0:T(8,128)(2,1)S(1)} all-to-all(bf16[16,64,512]{2,1,0:T(8,128)(2,1)S(1)} %bitcast.24), channel_id=1, replica_groups=mesh['a'=4,'b'=4,'y'=4,'x'=4,'c'=2] {'b','y'}, dimensions={0} | all-to-all | bytes 2097152 | tf_op jit(solution)/shard_map/all_to_all | solution.py:319
  166.0 4.6 %collective-permute-start.6 = (bf16[16,64,512]{2,1,0:T(8,128)(2,1)S(1)}, bf16[16,64,512]{2,1,0:T(8,128)(2,1)S(1)}, u32[]{:S(2)}, u32[]{:S(2)}) collective-permute-start(bf16[16,64,512]{2,1,0:T(8,128)(2,1)S(1)} %all_to_all.16.own_ref), channel_id=1, source_target_pairs={{0,1},{1,0},{2,3},{3,2},{4,5},{5,4},{6,7},{7,6},{8,9},{9,8},{10,11... | collective-permute-start | bytes 3145736 | tf_op jit(solution)/shard_map/ppermute | solution.py:287
  170.7 0.0 copy-done.2
  170.7 0.1 reshape.50
  170.9 0.7 copy.8
  171.6 0.1 copy.7
  171.7 0.6 select_reduce_fusion
  173.0 0.0 collective-permute-done.6.oth_ref
  173.0 2.1 %shard_map.63 = bf16[6,56,1024]{2,1,0:T(8,128)(2,1)} custom-call(s32[1]{0:T(128)} %bitcast.c_ref, bf16[16,64,512]{2,1,0:T(8,128)(2,1)S(1)} %all_to_all.16.own_ref, bf16[16,64,512]{2,1,0:T(8,128)(2,1)S(1)} %collective-permute-done.6.oth_ref), custom_call_target="tpu_custom_call" | custom-call | tf_op jit(solution)/shard_map/pallas_call | solution.py:273
  (4 shorter events, 0.0 us)
Async XLA Ops:
  0.6 1.3 copy-start
  2.0 1.3 copy-start.1
  5.6 10.0 %collective-permute-start = (bf16[6,56,512]{2,1,0:T(8,128)(2,1)S(1)}, bf16[6,56,512]{2,1,0:T(8,128)(2,1)S(1)}, u32[]{:S(2)}, u32[]{:S(2)}) collective-permute-start(bf16[6,56,512]{2,1,0:T(8,128)(2,1)S(1)} %get-tuple-element.10), channel_id=1, source_target_pairs={{0,1},{1,0},{2,3},{3,2},{4,5},{5,4},{6,7},{7,6},{8,9},{9,8},{10,11... | collective-permute-start | bytes 1032200 | tf_op jit(solution)/shard_map/ppermute | solution.py:287
  43.3 6.9 %collective-permute-start.1 = (bf16[1024,512]{1,0:T(8,128)(2,1)S(1)}, bf16[1024,512]{1,0:T(8,128)(2,1)S(1)}, u32[]{:S(2)}, u32[]{:S(2)}) collective-permute-start(bf16[1024,512]{1,0:T(8,128)(2,1)S(1)} %bitcast.21), channel_id=1, source_target_pairs={{0,1},{1,0},{2,3},{3,2},{4,5},{5,4},{6,7},{7,6},{8,9},{9,8},{10,11... | collective-permute-start | bytes 3145736 | tf_op jit(solution)/shard_map/ppermute | solution.py:287
  51.9 31.7 %all-to-all-start.1 = ((bf16[4,272,256]{2,1,0:T(8,128)(2,1)}), bf16[4,272,256]{2,1,0:T(8,128)(2,1)S(1)}, u32[]{:S(2)}, u32[]{:S(2)}) async-start(bf16[4,272,256]{2,1,0:T(8,128)(2,1)} %bitcast.5), calls=%async_computation.1 | async-start | bytes 1114112 | tf_op jit(solution)/shard_map/all_to_all | solution.py:314
  64.0 10.6 %collective-permute-start.2 = (f32[16,128]{1,0:T(8,128)S(1)}, f32[16,128]{1,0:T(8,128)S(1)}, u32[]{:S(2)}, u32[]{:S(2)}) collective-permute-start(f32[16,128]{1,0:T(8,128)S(1)} %get-tuple-element.12.t0_ref), channel_id=1, source_target_pairs={{0,2},{2,4},{4,6},{6,0},{1,3},{3,5},{5,7},{7,1},{8,10},{10,12},{12... | collective-permute-start | bytes 24584 | tf_op jit(solution)/shard_map/ppermute | solution.py:312
  67.1 7.4 %collective-permute-start.3 = (f32[16,128]{1,0:T(8,128)S(1)}, f32[16,128]{1,0:T(8,128)S(1)}, u32[]{:S(2)}, u32[]{:S(2)}) collective-permute-start(f32[16,128]{1,0:T(8,128)S(1)} %get-tuple-element.12.t0_ref), channel_id=1, source_target_pairs={{0,4},{2,6},{4,0},{6,2},{1,5},{3,7},{5,1},{7,3},{8,12},{10,14},{12... | collective-permute-start | bytes 24584 | tf_op jit(solution)/shard_map/ppermute | solution.py:312
  71.5 4.7 %collective-permute-start.4 = (f32[16,128]{1,0:T(8,128)S(1)}, f32[16,128]{1,0:T(8,128)S(1)}, u32[]{:S(2)}, u32[]{:S(2)}) collective-permute-start(f32[16,128]{1,0:T(8,128)S(1)} %get-tuple-element.12.t0_ref), channel_id=1, source_target_pairs={{0,6},{2,0},{4,2},{6,4},{1,7},{3,1},{5,3},{7,5},{8,14},{10,8},{12,... | collective-permute-start | bytes 24584 | tf_op jit(solution)/shard_map/ppermute | solution.py:312
  107.7 15.0 %collective-permute-start.5 = (bf16[4,288,256]{2,1,0:T(8,128)(2,1)S(1)}, bf16[4,288,256]{2,1,0:T(8,128)(2,1)S(1)}, u32[]{:S(2)}, u32[]{:S(2)}) collective-permute-start(bf16[4,288,256]{2,1,0:T(8,128)(2,1)S(1)} %bitcast.25), channel_id=1, source_target_pairs={{0,1},{1,0},{2,3},{3,2},{4,5},{5,4},{6,7},{7,6},{8,9},{9,8},{10,11... | collective-permute-start | bytes 1769480 | tf_op jit(solution)/shard_map/ppermute | solution.py:287
  133.5 37.2 %copy-start.2 = (s32[16,3]{0,1:T(4,128)S(1)}, s32[16,3]{0,1:T(4,128)}, u32[]{:S(2)}) copy-start(s32[16,3]{0,1:T(4,128)} %param.5) | copy-start | bytes 580
  166.0 6.9 %collective-permute-start.6 = (bf16[16,64,512]{2,1,0:T(8,128)(2,1)S(1)}, bf16[16,64,512]{2,1,0:T(8,128)(2,1)S(1)}, u32[]{:S(2)}, u32[]{:S(2)}) collective-permute-start(bf16[16,64,512]{2,1,0:T(8,128)(2,1)S(1)} %all_to_all.16.own_ref), channel_id=1, source_target_pairs={{0,1},{1,0},{2,3},{3,2},{4,5},{5,4},{6,7},{7,6},{8,9},{9,8},{10,11... | collective-permute-start | bytes 3145736 | tf_op jit(solution)/shard_map/ppermute | solution.py:287

commit v2 on v1

v2 whole, which is shorter than its diff:
```python
import itertools
import math

import jax
import jax.numpy as jnp
from jax import lax
from jax.experimental import pallas as pl
from jax.experimental.pallas import tpu as pltpu
from jax.sharding import Mesh
from jax.sharding import PartitionSpec as P

D = 3584
FF = 1024
HALF = FF // 2
BLK = 256
SHARD = 56
ROWS = 64
CHUNK = 272

MU = 0.95
COEF_P = 3.4445
COEF_Q = -4.775
COEF_T = 2.0315


F32 = jnp.float32
BF16 = jnp.bfloat16
VMEM = pl.BlockSpec(memory_space=pltpu.VMEM)
SMEM = pl.BlockSpec(memory_space=pltpu.SMEM)


def params(mib):
    return pltpu.CompilerParams(vmem_limit_bytes=mib * 1024 * 1024)


def dot(a, b):
    return jnp.dot(a, b, preferred_element_type=F32)


def dot_rows(a, b):
    return lax.dot_general(a, b, (((0,), (0,)), ((), ())), preferred_element_type=F32)


def blend_kernel(c_ref, grad_ref, mom_ref, new_ref, keep_ref, send_ref, sum_ref):
    first = c_ref[0] == 0
    grad = grad_ref[0]
    new = MU * mom_ref[0] + grad
    new_ref[0] = new
    blended = (grad + MU * new).astype(BF16)
    left, right = blended[:, :HALF], blended[:, HALF:]
    keep_ref[0] = jnp.where(first, left, right)
    send_ref[0] = jnp.where(first, right, left)
    rounded = blended.astype(F32)
    total = jnp.sum(jnp.sum(rounded * rounded, axis=0, keepdims=True), axis=1, keepdims=True)
    sum_ref[0] = jnp.broadcast_to(total, (8, 128))


def blend(ctl, grad, momentum):
    count = grad.shape[0]
    full = pl.BlockSpec((1, SHARD, FF), lambda i: (i, 0, 0))
    half = pl.BlockSpec((1, SHARD, HALF), lambda i: (i, 0, 0))
    return pl.pallas_call(
        blend_kernel,
        grid=(count,),
        in_specs=[SMEM, full, full],
        out_specs=[full, half, half, pl.BlockSpec((1, 8, 128), lambda i: (i, 0, 0))],
        out_shape=[
            jax.ShapeDtypeStruct((count, SHARD, FF), F32),
            jax.ShapeDtypeStruct((count, SHARD, HALF), BF16),
            jax.ShapeDtypeStruct((count, SHARD, HALF), BF16),
            jax.ShapeDtypeStruct((count, 8, 128), F32),
        ],
        compiler_params=params(16),
    )(ctl, grad, momentum)


def pack_kernel(c_ref, keep_ref, recv_ref, sum_ref, out_ref):
    c = c_ref[0]
    lane = lax.broadcasted_iota(jnp.int32, (8, 128), 1)
    sums = jnp.zeros((8, 128), F32)
    for k in range(3):
        for g in range(2):
            sums = jnp.where(lane == (2 * c + g) * 3 + k, sum_ref[g * 3 + k], sums)
    high = sums.astype(BF16).astype(F32)
    note = jnp.concatenate([high, sums - high, jnp.zeros((8, HALF - 256), F32)], axis=1)
    note = jnp.concatenate([note] * (SHARD // 8), axis=0).astype(BF16)
    for q in range(4):
        for k in range(3):
            i = (q % 2) * 3 + k
            out_ref[k * 4 + q] = jnp.where(c == q // 2, keep_ref[i], recv_ref[i])
        out_ref[12 + q] = note


def pack(ctl, keep, recv, sums):
    return pl.pallas_call(
        pack_kernel,
        in_specs=[SMEM, VMEM, VMEM, VMEM],
        out_specs=VMEM,
        out_shape=jax.ShapeDtypeStruct((16, SHARD, HALF), BF16),
        compiler_params=params(16),
    )(ctl, keep, recv, sums)


def fill(ref, scratch):
    pad = jnp.zeros((ROWS - SHARD, HALF), F32)
    for i in range(16):
        block = jnp.concatenate([ref[i].astype(F32), pad], axis=0)
        scratch[i * ROWS : (i + 1) * ROWS] = block.astype(BF16)


def index_grid(shape):
    return lax.broadcasted_iota(jnp.int32, shape, 0), lax.broadcasted_iota(jnp.int32, shape, 1)


def split(value):
    high = value.astype(BF16).astype(F32)
    return jnp.concatenate([high, value - high], axis=1)


def gram_kernel(c_ref, own_ref, oth_ref, p0_ref, p1_ref, p2_ref, p3_ref, xs, ys, out_ref):
    first = c_ref[0] == 0
    fill(own_ref, xs)
    fill(oth_ref, ys)
    row, col = index_grid((BLK, BLK))
    x0, x1 = xs[:, :BLK], xs[:, BLK:]
    y0, y1 = ys[:, :BLK], ys[:, BLK:]
    g00, g11 = dot_rows(x0, x0), dot_rows(x1, x1)
    diag1 = jnp.sum(jnp.where(row == col, g11, 0.0), axis=0, keepdims=True)
    out_ref[0:BLK] = jnp.where(row <= col, g00, g11).astype(BF16)
    out_ref[BLK : 2 * BLK] = dot_rows(x0, x1).astype(BF16)
    out_ref[2 * BLK : 3 * BLK] = dot_rows(x0, jnp.where(first, y0, y1)).astype(BF16)
    out_ref[3 * BLK : 4 * BLK] = dot_rows(x1, jnp.where(first, y1, y0)).astype(BF16)
    out_ref[4 * BLK :] = jnp.broadcast_to(diag1, (4 * CHUNK - 4 * BLK, BLK)).astype(BF16)
    note = xs[0:16, :BLK].astype(F32)
    for i in range(1, 16):
        note = note + xs[i * ROWS : i * ROWS + 16, :BLK].astype(F32)
    note = split(note[:, :128] + note[:, 128:])
    idle = c_ref[1] == 1
    for j, ref in enumerate((p0_ref, p1_ref, p2_ref, p3_ref)):
        start = pl.multiple_of(lax.rem(c_ref[2] + j, 4) * CHUNK, 16)
        ref[...] = out_ref[pl.ds(start, CHUNK)]
        ref[:16] = jnp.where(idle, note, ref[:16].astype(F32)).astype(BF16)


def partial_gram(ctl, own, oth):
    return pl.pallas_call(
        gram_kernel,
        in_specs=[SMEM, VMEM, VMEM],
        out_specs=[VMEM] * 4,
        out_shape=[jax.ShapeDtypeStruct((CHUNK, BLK), BF16)] * 4,
        scratch_shapes=[pltpu.VMEM((16 * ROWS, HALF), BF16)] * 2
        + [pltpu.VMEM((4 * CHUNK, BLK), BF16)],
        compiler_params=params(32),
    )(ctl, own, oth)


def sum_kernel(c_ref, p0_ref, p1_ref, p2_ref, p3_ref, out_ref):
    total = p0_ref[...].astype(F32) + p1_ref[...].astype(F32)
    total = total + (p2_ref[...].astype(F32) + p3_ref[...].astype(F32))
    out_ref[...] = total.astype(BF16)
    y = c_ref[3]
    note = p0_ref[:16].astype(F32)
    for j, ref in enumerate((p1_ref, p2_ref, p3_ref)):
        note = jnp.where(y == j + 1, ref[:16].astype(F32), note)
    out_ref[:16] = jnp.where(c_ref[1] == 1, note, total[:16]).astype(BF16)


def sum_parts(ctl, parts):
    return pl.pallas_call(
        sum_kernel,
        in_specs=[SMEM] + [VMEM] * 4,
        out_specs=VMEM,
        out_shape=jax.ShapeDtypeStruct((CHUNK, BLK), BF16),
        compiler_params=params(16),
    )(ctl, *parts)


def collect_kernel(c_ref, p0_ref, p1_ref, p2_ref, p3_ref, out_ref):
    for j, ref in enumerate((p0_ref, p1_ref, p2_ref, p3_ref)):
        out_ref[lax.rem(c_ref[2] + 4 - j, 4)] = ref[...]


def collect(ctl, parts):
    return pl.pallas_call(
        collect_kernel,
        in_specs=[SMEM] + [VMEM] * 4,
        out_specs=VMEM,
        out_shape=jax.ShapeDtypeStruct((4, CHUNK, BLK), BF16),
        compiler_params=params(16),
    )(ctl, *parts)


def unpack(ref):
    blocks, at = [], 0
    for _ in range(4):
        pieces, need = [], BLK
        while need:
            chunk, offset = divmod(at, CHUNK)
            take = min(need, CHUNK - offset)
            pieces.append(ref[chunk, offset : offset + take])
            at, need = at + take, need - take
        piece = pieces[0] if len(pieces) == 1 else jnp.concatenate(pieces, axis=0)
        blocks.append(piece.astype(F32))
    offset = at - 3 * CHUNK
    return blocks, ref[3, offset : offset + 16].astype(F32)[0:1]


def polynomial_kernel(
    c_ref, own_ref, oth_ref, xo_ref, xt_ref, out_ref, xs, ys, a32, ab, m32, mb, c32, cb, gb, w32, nb, wb
):
    first = c_ref[0] == 0
    idle = c_ref[1] == 1
    fill(xo_ref, xs)
    fill(xt_ref, ys)
    row, col = index_grid((BLK, BLK))
    (d_o, o01, p2, p3), e_o = unpack(own_ref)
    (d_t, t01, r2, r3), e_t = unpack(oth_ref)

    trace = jnp.sum(jnp.where(row == col, d_o + d_t, 0.0), axis=0, keepdims=True) + (e_o + e_t)
    scale = lax.rsqrt(jnp.sum(trace, axis=1, keepdims=True))
    square = scale * scale

    def put(i, j, value):
        value = value * square
        a32[i * BLK : (i + 1) * BLK, j * BLK : (j + 1) * BLK] = value
        ab[i * BLK : (i + 1) * BLK, j * BLK : (j + 1) * BLK] = value.astype(BF16)

    def put_pair(i, j, value, turned):
        put(i, j, value)
        put(j, i, turned)

    for base, packed, edge, off in ((0, d_o, e_o, o01), (2, d_t, e_t, t01)):
        turned = packed.T
        put(base, base, jnp.where(row <= col, packed, turned))
        upper = jnp.where(row == col, jnp.broadcast_to(edge, (BLK, BLK)), turned)
        put(base + 1, base + 1, jnp.where(row > col, packed, upper))
        put_pair(base, base + 1, off, off.T)
    p2t, p3t, r2t, r3t = p2.T, p3.T, r2.T, r3.T
    put_pair(0, 2, jnp.where(first, p2, r2t), jnp.where(first, p2t, r2))
    put_pair(0, 3, jnp.where(first, r3t, p2), jnp.where(first, r3, p2t))
    put_pair(1, 2, jnp.where(first, r2t, p3), jnp.where(first, r2, p3t))
    put_pair(1, 3, jnp.where(first, p3, r3t), jnp.where(first, p3t, r3))

    blocks = [slice(i * BLK, (i + 1) * BLK) for i in range(4)]
    for s in blocks:
        poly = COEF_Q * a32[s] + COEF_T * dot(ab[s], ab[...])
        m32[s] = poly[:, :HALF]
        mb[s] = poly.astype(BF16)
    for s in blocks:
        prod = COEF_P * a32[s] + dot(ab[s], mb[...])
        c32[s] = prod
        cb[s] = prod.astype(BF16)
    for s in blocks:
        gram = COEF_P * c32[s] + dot(cb[s], mb[...])
        c32[s] = gram
        gb[s] = gram.astype(BF16)
    for s in blocks:
        poly = COEF_Q * c32[s, :HALF] + COEF_T * dot(gb[s], gb[:, :HALF])
        nb[s] = poly.astype(BF16)
        w32[s] = COEF_P * (poly + m32[s])
    for s in blocks:
        wb[s] = (w32[s] + dot(mb[s], nb[...])).astype(BF16)

    notes = []
    for j in range(4):
        at = lax.rem(c_ref[2] + 4 - j, 4)
        both = own_ref[at, :16].astype(F32) + oth_ref[at, :16].astype(F32)
        notes.append((both[:, :128] + both[:, 128:])[0:1])
    note = jnp.concatenate(notes, axis=1)
    high = note.astype(BF16).astype(F32)
    spot = lax.broadcasted_iota(jnp.int32, (ROWS, HALF), 0)
    note = jnp.where(spot < 16, high, note - high)
    factor = scale * math.sqrt(D)
    for s in blocks:
        own = xs[s]
        value = dot(own, wb[:HALF]) + dot(ys[s], wb[HALF:])
        value = (value + (COEF_P * COEF_P) * own.astype(F32)) * factor
        for i in range(BLK // ROWS):
            piece = jnp.where(idle, note, value[i * ROWS : (i + 1) * ROWS])
            out_ref[s.start // ROWS + i] = piece[:SHARD].astype(BF16)


def polynomial(core, own_gram, oth_gram, own, oth):
    square = (FF, FF)
    tall = (FF, HALF)
    return pl.pallas_call(
        polynomial_kernel,
        in_specs=[SMEM, VMEM, VMEM, VMEM, VMEM],
        out_specs=VMEM,
        out_shape=jax.ShapeDtypeStruct((16, SHARD, HALF), BF16),
        scratch_shapes=[
            pltpu.VMEM((16 * ROWS, HALF), BF16),
            pltpu.VMEM((16 * ROWS, HALF), BF16),
            pltpu.VMEM(square, F32),
            pltpu.VMEM(square, BF16),
            pltpu.VMEM(tall, F32),
            pltpu.VMEM(square, BF16),
            pltpu.VMEM(square, F32),
            pltpu.VMEM(square, BF16),
            pltpu.VMEM(square, BF16),
            pltpu.VMEM(tall, F32),
            pltpu.VMEM(tall, BF16),
            pltpu.VMEM(tall, BF16),
        ],
        compiler_params=params(48),
    )(core, own_gram, oth_gram, own, oth)


def join_kernel(c_ref, own_ref, oth_ref, out_ref):
    first = c_ref[0] == 0
    own, oth = own_ref[0], oth_ref[0]
    out_ref[0, :, :HALF] = jnp.where(first, own, oth)
    out_ref[0, :, HALF:] = jnp.where(first, oth, own)


def join(core, own, oth):
    def slot(i, c):
        return ((i % 3) * 4 + 2 * c[0] + i // 3, 0, 0)

    return pl.pallas_call(
        join_kernel,
        grid_spec=pltpu.PrefetchScalarGridSpec(
            num_scalar_prefetch=1,
            grid=(6,),
            in_specs=[pl.BlockSpec((1, SHARD, HALF), slot)] * 2,
            out_specs=pl.BlockSpec((1, SHARD, FF), lambda i, c: (i, 0, 0)),
        ),
        out_shape=jax.ShapeDtypeStruct((6, SHARD, FF), BF16),
        compiler_params=params(16),
    )(core, own, oth)


def swap(value):
    return lax.ppermute(value, "c", [(0, 1), (1, 0)])


def owner_rms(notes, owners):
    norms = jnp.sum(notes[:, 0].astype(F32) + notes[:, 16].astype(F32), axis=0)
    norms = norms.reshape(4, 128)[:, :12].reshape(4, 4, 3)
    x = lax.axis_index("x")
    table = owners.reshape(4, 4, 3)
    turned = jnp.stack([lax.dynamic_index_in_dim(table, (x - j) % 4, 0, False) for j in range(4)])
    me = (lax.axis_index("a") * 4 + lax.axis_index("b")) * 4 + lax.axis_index("y")
    return jnp.sqrt(jnp.sum(jnp.where(turned == me, norms, 0.0)) / (D * FF)).reshape(1)


def between(value, shift, idle_pair):
    pairs = []
    for a, b, y, x in itertools.product(range(4), repeat=4):
        target = ((a + shift) % 4, b, y, x) if b < 3 else idle_pair(a, y, x)
        if target is not None:
            index = [((h * 4 + i) * 4 + j) * 4 + k for h, i, j, k in ((a, b, y, x), target)]
            pairs.append(tuple(index))
    return lax.ppermute(value, ("a", "b", "y", "x"), pairs)


def shards(grad, momentum, owners):
    shape = grad.shape
    index = [lax.axis_index("c"), lax.axis_index("b") == 3, lax.axis_index("a"), lax.axis_index("y")]
    ctl = jnp.stack([i.astype(jnp.int32) for i in index])
    flat = (6, SHARD, FF)
    grad = pltpu.with_memory_space_constraint(grad.reshape(flat), pltpu.HBM)
    momentum = pltpu.with_memory_space_constraint(momentum.reshape(flat), pltpu.HBM)
    momentum_new, keep, send, sums = blend(ctl, grad, momentum)
    packed = pack(ctl, keep, swap(send), sums)
    own = lax.all_to_all(packed, ("b", "y"), 0, 0, tiled=True)
    oth = swap(own)
    partial = partial_gram(ctl, own, oth)
    parts = [partial[0]]
    for j in (1, 2, 3):
        far = lambda a, y, x, j=j: ((a + j) % 4, 3, y, x) if y == j else None
        parts.append(between(partial[j], j, far))
    mine = sum_parts(ctl, parts)
    parts = [mine]
    for j in (1, 2, 3):
        parts.append(between(mine, j, lambda a, y, x, j=j: (a, 3, y, (x + j) % 4)))
    own_gram = collect(ctl, parts)
    oth_gram = swap(own_gram)
    finished = polynomial(ctl, own_gram, oth_gram, own, oth)
    back = lax.all_to_all(finished, ("b", "y"), 0, 0, tiled=True)
    update = join(ctl, back, swap(back))
    owned_rms = owner_rms(back[12:], owners)
    return (momentum_new.reshape(shape), update.reshape(shape), owned_rms)


def solution(mesh):
    fine = Mesh(mesh.devices.reshape(4, 4, 4, 4, 2), ("a", "b", "y", "x", "c"))
    rows = ("a", "b", "y")
    wide = P(("x", "c"), None, rows, None)
    return jax.shard_map(
        shards, mesh=fine, in_specs=(wide, wide, P()), out_specs=(wide, wide, P(rows)), check_vma=False
    )
```

time: 177 us -> 170 us (0.960)
  blocking collectives: 84.2 us -> 52.7 us
  waiting for transfers between devices: 14.2 us -> 29.1 us
  starting transfers between devices: 54 us -> 61.1 us
  Pallas kernels: 16.9 us -> 22.3 us
  local copies, waits for them, and re-layouts: 3.58 us -> 0.81 us
    ppermute x3 -> x6, starting transfers between devices: 10.5 us -> 41.5 us  [between(): return lax.ppermute(value, ('a', 'b', 'y', 'x'), pairs)]
    all_gather x1 -> x0, blocking collectives: 24 us -> none  [shards(): own_gram = lax.all_gather(mine, 'a', axis=0)]
    ppermute x3 -> x6, waiting for transfers between devices: 1.61 us -> 24.4 us  [between(): return lax.ppermute(value, ('a', 'b', 'y', 'x'), pairs)]
    all_to_all x1 -> x0, starting transfers between devices: 12.1 us -> none  [shards(): lax.all_to_all(partial.reshape(4, CHUNK, BLK), 'a', 0, 0, tiled=True)]
    ppermute x4, starting transfers between devices: 31.4 us -> 19.6 us  [swap(): return lax.ppermute(value, 'c', [(0, 1), (1, 0)])]
    all_to_all x2, blocking collectives: 60.2 us -> 52.7 us  [the longest x1 27 us: shards(): back = lax.all_to_all(finished, ('b', 'y'), 0, 0, tiled=True)]
    all_to_all x1 -> x0, waiting for transfers between devices: 7.44 us -> none  [shards(): lax.all_to_all(partial.reshape(4, CHUNK, BLK), 'a', 0, 0, tiled=True)]
    unnamed x7 -> x2, local copies, waits for them, and re-layouts: 3.37 us -> 0.01 us
  transfers between devices with their start and end apart: 8 -> 10, of which waited for: 5 -> 6; matrix products, arithmetic and copies ran while one was open for 1% -> 1% of each run, Pallas kernels for 0% -> 0%
where the time goes in v2:
time: 170 us
  starting transfers between devices  61.1 us (36%)
  blocking collectives  52.7 us (31%)
  waiting for transfers between devices  29.1 us (17%)
  Pallas kernels  22.3 us (13%)
  between operations  2.7 us (2%)
    ppermute x6, starting transfers between devices, between(): return lax.ppermute(value, ('a', 'b', 'y', 'x'), pairs)  41.5 us
    all_to_all x1, blocking collectives, shards(): back = lax.all_to_all(finished, ('b', 'y'), 0, 0, tiled=True)  27 us
    all_to_all x1, blocking collectives, shards(): own = lax.all_to_all(packed, ('b', 'y'), 0, 0, tiled=True)  25.7 us
    ppermute x6, waiting for transfers between devices, between(): return lax.ppermute(value, ('a', 'b', 'y', 'x'), pairs)  24.4 us
    ppermute x4, starting transfers between devices, swap(): return lax.ppermute(value, 'c', [(0, 1), (1, 0)])  19.6 us
    pallas_call x1, Pallas kernels, polynomial(): pl.pallas_call(polynomial_kernel, in_specs=[SMEM, VMEM, VMEM, VMEM, VMEM]...  11.5 us
    pallas_call x1, Pallas kernels, blend(): pl.pallas_call(blend_kernel, grid=(count,), in_specs=[SMEM, full, full],...  4.95 us
    ppermute x4, waiting for transfers between devices, swap(): return lax.ppermute(value, 'c', [(0, 1), (1, 0)])  4.72 us
  transfers between devices with their start and end apart: 10, of which 6 were waited for; matrix products, arithmetic and copies ran while one was open for 1% of the time, Pallas kernels for 0%

profile of v2, /device:TPU:1, one launch (start us, length us, event | category | flops | bytes accessed | tf_op | source)
XLA Modules:
  0.0 169.5 jit_solution(5811133399646596103)
XLA Ops:
  0.6 0.1 pad_add_fusion.c_ref
  0.7 5.0 %shard_map.58 = (f32[6,56,1024]{2,1,0:T(8,128)}, bf16[6,56,512]{2,1,0:T(8,128)(2,1)S(1)}, bf16[6,56,512]{2,1,0:T(8,128)(2,1)S(1)}, f32[6,8,128]{2,1,0:T(8,128)S(1)}) custom-call(s32[4]{0:T(128)S(1)} %pad_add_fusion.c_ref, f32[6,56,1024]{2,1,0:T(8,128)} %bitcast.12, f32[6,56,1024]{2,1,0:T(8,128)} %bitcast.13), custom_call_target="tpu_custom_call" | custom-call | tf_op jit(solution)/shard_map/pallas_call | solution.py:62
  5.7 8.8 %collective-permute-start = (bf16[6,56,512]{2,1,0:T(8,128)(2,1)S(1)}, bf16[6,56,512]{2,1,0:T(8,128)(2,1)S(1)}, u32[]{:S(2)}, u32[]{:S(2)}) collective-permute-start(bf16[6,56,512]{2,1,0:T(8,128)(2,1)S(1)} %get-tuple-element.13), channel_id=1, source_target_pairs={{0,1},{1,0},{2,3},{3,2},{4,5},{5,4},{6,7},{7,6},{8,9},{9,8},{10,11... | collective-permute-start | bytes 1032200 | tf_op jit(solution)/shard_map/ppermute | solution.py:334
  14.5 1.3 collective-permute-done.recv_ref
  15.7 0.6 shard_map.59
  16.3 25.7 %all_to_all.10.own_ref.xo_ref = bf16[16,56,512]{2,1,0:T(8,128)(2,1)S(1)} all-to-all(bf16[16,56,512]{2,1,0:T(8,128)(2,1)S(1)} %shard_map.59), channel_id=1, replica_groups=mesh['a'=4,'b'=4,'y'=4,'x'=4,'c'=2] {'b','y'}, dimensions={0} | all-to-all | bytes 1835008 | tf_op jit(solution)/shard_map/all_to_all | solution.py:366
  42.0 4.1 %collective-permute-start.1 = (bf16[16,56,512]{2,1,0:T(8,128)(2,1)S(1)}, bf16[16,56,512]{2,1,0:T(8,128)(2,1)S(1)}, u32[]{:S(2)}, u32[]{:S(2)}) collective-permute-start(bf16[16,56,512]{2,1,0:T(8,128)(2,1)S(1)} %all_to_all.10.own_ref.xo_ref), channel_id=1, source_target_pairs={{0,1},{1,0},{2,3},{3,2},{4,5},{5,4},{6,7},{7,6},{8,9},{9,8},{10,11... | collective-permute-start | bytes 2752520 | tf_op jit(solution)/shard_map/ppermute | solution.py:334
  46.1 2.1 %collective-permute-done.1.oth_ref.xt_ref = bf16[16,56,512]{2,1,0:T(8,128)(2,1)S(1)} collective-permute-done((bf16[16,56,512]{2,1,0:T(8,128)(2,1)S(1)}, bf16[16,56,512]{2,1,0:T(8,128)(2,1)S(1)}, u32[]{:S(2)}, u32[]{:S(2)}) %collective-permute-start.1) | collective-permute-done | bytes 917536 | tf_op jit(solution)/shard_map/ppermute | solution.py:334
  48.2 1.5 shard_map.60
  49.7 8.8 %collective-permute-start.2 = (bf16[272,256]{1,0:T(8,128)(2,1)S(1)}, bf16[272,256]{1,0:T(8,128)(2,1)S(1)}, u32[]{:S(2)}, u32[]{:S(2)}) collective-permute-start(bf16[272,256]{1,0:T(8,128)(2,1)S(1)} %get-tuple-element.16), channel_id=1, source_target_pairs={{0,128},{2,130},{4,132},{6,134},{8,136},{10,138},{12,140},{14,142}... | collective-permute-start | bytes 417800 | tf_op jit(solution)/shard_map/ppermute | solution.py:354
  58.5 7.9 %collective-permute-start.3 = (bf16[272,256]{1,0:T(8,128)(2,1)S(1)}, bf16[272,256]{1,0:T(8,128)(2,1)S(1)}, u32[]{:S(2)}, u32[]{:S(2)}) collective-permute-start(bf16[272,256]{1,0:T(8,128)(2,1)S(1)} %get-tuple-element.17), channel_id=1, source_target_pairs={{0,256},{2,258},{4,260},{6,262},{8,264},{10,266},{12,268},{14,270}... | collective-permute-start | bytes 417800 | tf_op jit(solution)/shard_map/ppermute | solution.py:354
  66.5 5.2 %collective-permute-start.4 = (bf16[272,256]{1,0:T(8,128)(2,1)S(1)}, bf16[272,256]{1,0:T(8,128)(2,1)S(1)}, u32[]{:S(2)}, u32[]{:S(2)}) collective-permute-start(bf16[272,256]{1,0:T(8,128)(2,1)S(1)} %get-tuple-element.18), channel_id=1, source_target_pairs={{0,384},{2,386},{4,388},{6,390},{8,392},{10,394},{12,396},{14,398}... | collective-permute-start | bytes 417800 | tf_op jit(solution)/shard_map/ppermute | solution.py:354
  71.7 0.0 collective-permute-done.2.p1_ref
  71.7 7.5 %collective-permute-done.3.p2_ref = bf16[272,256]{1,0:T(8,128)(2,1)S(1)} collective-permute-done((bf16[272,256]{1,0:T(8,128)(2,1)S(1)}, bf16[272,256]{1,0:T(8,128)(2,1)S(1)}, u32[]{:S(2)}, u32[]{:S(2)}) %collective-permute-start.3) | collective-permute-done | bytes 139296 | tf_op jit(solution)/shard_map/ppermute | solution.py:354
  79.2 2.6 %collective-permute-done.4.p3_ref = bf16[272,256]{1,0:T(8,128)(2,1)S(1)} collective-permute-done((bf16[272,256]{1,0:T(8,128)(2,1)S(1)}, bf16[272,256]{1,0:T(8,128)(2,1)S(1)}, u32[]{:S(2)}, u32[]{:S(2)}) %collective-permute-start.4) | collective-permute-done | bytes 139296 | tf_op jit(solution)/shard_map/ppermute | solution.py:354
  81.8 0.6 shard_map.61.p0_ref
  82.4 10.7 %collective-permute-start.5 = (bf16[272,256]{1,0:T(8,128)(2,1)S(1)}, bf16[272,256]{1,0:T(8,128)(2,1)S(1)}, u32[]{:S(2)}, u32[]{:S(2)}) collective-permute-start(bf16[272,256]{1,0:T(8,128)(2,1)S(1)} %shard_map.61.p0_ref), channel_id=1, source_target_pairs={{0,128},{2,130},{4,132},{6,134},{8,136},{10,138},{12,140},{14,142}... | collective-permute-start | bytes 417800 | tf_op jit(solution)/shard_map/ppermute | solution.py:354
  93.1 6.2 %collective-permute-start.6 = (bf16[272,256]{1,0:T(8,128)(2,1)S(1)}, bf16[272,256]{1,0:T(8,128)(2,1)S(1)}, u32[]{:S(2)}, u32[]{:S(2)}) collective-permute-start(bf16[272,256]{1,0:T(8,128)(2,1)S(1)} %shard_map.61.p0_ref), channel_id=1, source_target_pairs={{0,256},{2,258},{4,260},{6,262},{8,264},{10,266},{12,268},{14,270}... | collective-permute-start | bytes 417800 | tf_op jit(solution)/shard_map/ppermute | solution.py:354
  99.2 2.8 %collective-permute-start.7 = (bf16[272,256]{1,0:T(8,128)(2,1)S(1)}, bf16[272,256]{1,0:T(8,128)(2,1)S(1)}, u32[]{:S(2)}, u32[]{:S(2)}) collective-permute-start(bf16[272,256]{1,0:T(8,128)(2,1)S(1)} %shard_map.61.p0_ref), channel_id=1, source_target_pairs={{0,384},{2,386},{4,388},{6,390},{8,392},{10,394},{12,396},{14,398}... | collective-permute-start | bytes 417800 | tf_op jit(solution)/shard_map/ppermute | solution.py:354
  102.0 0.0 collective-permute-done.5.p1_ref
  102.0 14.3 %collective-permute-done.6.p2_ref = bf16[272,256]{1,0:T(8,128)(2,1)S(1)} collective-permute-done((bf16[272,256]{1,0:T(8,128)(2,1)S(1)}, bf16[272,256]{1,0:T(8,128)(2,1)S(1)}, u32[]{:S(2)}, u32[]{:S(2)}) %collective-permute-start.6) | collective-permute-done | bytes 139296 | tf_op jit(solution)/shard_map/ppermute | solution.py:354
  116.3 0.0 collective-permute-done.7.p3_ref
  116.3 0.6 shard_map.62.own_ref
  116.9 2.6 %collective-permute-start.8 = (bf16[4,272,256]{2,1,0:T(8,128)(2,1)S(1)}, bf16[4,272,256]{2,1,0:T(8,128)(2,1)S(1)}, u32[]{:S(2)}, u32[]{:S(2)}) collective-permute-start(bf16[4,272,256]{2,1,0:T(8,128)(2,1)S(1)} %shard_map.62.own_ref), channel_id=1, source_target_pairs={{0,1},{1,0},{2,3},{3,2},{4,5},{5,4},{6,7},{7,6},{8,9},{9,8},{10,11... | collective-permute-start | bytes 1671176 | tf_op jit(solution)/shard_map/ppermute | solution.py:334
  119.5 1.4 collective-permute-done.8.oth_ref
  120.9 11.5 %shard_map.63 = bf16[16,56,512]{2,1,0:T(8,128)(2,1)S(1)} custom-call(s32[4]{0:T(128)S(1)} %pad_add_fusion.c_ref, bf16[4,272,256]{2,1,0:T(8,128)(2,1)S(1)} %shard_map.62.own_ref, bf16[4,272,256]{2,1,0:T(8,128)(2,1)S(1)} %collective-permute-done.8.oth_ref, bf16[16,56,512]{2,1,0:T(8,128)(2,1)S(1)} %all_to_all.10.own_ref.xo_ref, ...), custom_call_target="tpu_custom_call" | custom-call | tf_op jit(solution)/shard_map/pallas_call | solution.py:286
  132.4 0.0 copy-start
  132.4 27.0 %all_to_all.11.own_ref = bf16[16,56,512]{2,1,0:T(8,128)(2,1)S(1)} all-to-all(bf16[16,56,512]{2,1,0:T(8,128)(2,1)S(1)} %shard_map.63), channel_id=1, replica_groups=mesh['a'=4,'b'=4,'y'=4,'x'=4,'c'=2] {'b','y'}, dimensions={0} | all-to-all | bytes 1835008 | tf_op jit(solution)/shard_map/all_to_all | solution.py:380
  159.4 4.1 %collective-permute-start.9 = (bf16[16,56,512]{2,1,0:T(8,128)(2,1)S(1)}, bf16[16,56,512]{2,1,0:T(8,128)(2,1)S(1)}, u32[]{:S(2)}, u32[]{:S(2)}) collective-permute-start(bf16[16,56,512]{2,1,0:T(8,128)(2,1)S(1)} %all_to_all.11.own_ref), channel_id=1, source_target_pairs={{0,1},{1,0},{2,3},{3,2},{4,5},{5,4},{6,7},{7,6},{8,9},{9,8},{10,11... | collective-permute-start | bytes 2752520 | tf_op jit(solution)/shard_map/ppermute | solution.py:334
  163.6 0.0 copy-done
  163.6 0.1 reshape.39
  163.7 0.1 copy.13
  163.8 0.1 stack.42
  163.9 0.1 copy.12
  164.0 0.1 stack.41
  164.1 0.1 copy.11
  164.2 0.1 stack.40
  164.3 0.1 copy.10
  164.4 0.1 stack.39
  164.5 0.6 select_reduce_fusion
  165.8 0.0 collective-permute-done.9.oth_ref
  165.8 2.6 %shard_map.64 = bf16[6,56,1024]{2,1,0:T(8,128)(2,1)} custom-call(s32[4]{0:T(128)S(1)} %pad_add_fusion.c_ref, bf16[16,56,512]{2,1,0:T(8,128)(2,1)S(1)} %all_to_all.11.own_ref, bf16[16,56,512]{2,1,0:T(8,128)(2,1)S(1)} %collective-permute-done.9.oth_ref), custom_call_target="tpu_custom_call" | custom-call | tf_op jit(solution)/shard_map/pallas_call | solution.py:320
  (2 shorter events, 0.0 us)
Async XLA Ops:
  5.7 10.0 %collective-permute-start = (bf16[6,56,512]{2,1,0:T(8,128)(2,1)S(1)}, bf16[6,56,512]{2,1,0:T(8,128)(2,1)S(1)}, u32[]{:S(2)}, u32[]{:S(2)}) collective-permute-start(bf16[6,56,512]{2,1,0:T(8,128)(2,1)S(1)} %get-tuple-element.13), channel_id=1, source_target_pairs={{0,1},{1,0},{2,3},{3,2},{4,5},{5,4},{6,7},{7,6},{8,9},{9,8},{10,11... | collective-permute-start | bytes 1032200 | tf_op jit(solution)/shard_map/ppermute | solution.py:334
  42.0 6.2 %collective-permute-start.1 = (bf16[16,56,512]{2,1,0:T(8,128)(2,1)S(1)}, bf16[16,56,512]{2,1,0:T(8,128)(2,1)S(1)}, u32[]{:S(2)}, u32[]{:S(2)}) collective-permute-start(bf16[16,56,512]{2,1,0:T(8,128)(2,1)S(1)} %all_to_all.10.own_ref.xo_ref), channel_id=1, source_target_pairs={{0,1},{1,0},{2,3},{3,2},{4,5},{5,4},{6,7},{7,6},{8,9},{9,8},{10,11... | collective-permute-start | bytes 2752520 | tf_op jit(solution)/shard_map/ppermute | solution.py:334
  49.7 22.0 %collective-permute-start.2 = (bf16[272,256]{1,0:T(8,128)(2,1)S(1)}, bf16[272,256]{1,0:T(8,128)(2,1)S(1)}, u32[]{:S(2)}, u32[]{:S(2)}) collective-permute-start(bf16[272,256]{1,0:T(8,128)(2,1)S(1)} %get-tuple-element.16), channel_id=1, source_target_pairs={{0,128},{2,130},{4,132},{6,134},{8,136},{10,138},{12,140},{14,142}... | collective-permute-start | bytes 417800 | tf_op jit(solution)/shard_map/ppermute | solution.py:354
  58.5 20.7 %collective-permute-start.3 = (bf16[272,256]{1,0:T(8,128)(2,1)S(1)}, bf16[272,256]{1,0:T(8,128)(2,1)S(1)}, u32[]{:S(2)}, u32[]{:S(2)}) collective-permute-start(bf16[272,256]{1,0:T(8,128)(2,1)S(1)} %get-tuple-element.17), channel_id=1, source_target_pairs={{0,256},{2,258},{4,260},{6,262},{8,264},{10,266},{12,268},{14,270}... | collective-permute-start | bytes 417800 | tf_op jit(solution)/shard_map/ppermute | solution.py:354
  66.5 15.3 %collective-permute-start.4 = (bf16[272,256]{1,0:T(8,128)(2,1)S(1)}, bf16[272,256]{1,0:T(8,128)(2,1)S(1)}, u32[]{:S(2)}, u32[]{:S(2)}) collective-permute-start(bf16[272,256]{1,0:T(8,128)(2,1)S(1)} %get-tuple-element.18), channel_id=1, source_target_pairs={{0,384},{2,386},{4,388},{6,390},{8,392},{10,394},{12,396},{14,398}... | collective-permute-start | bytes 417800 | tf_op jit(solution)/shard_map/ppermute | solution.py:354
  82.4 19.6 %collective-permute-start.5 = (bf16[272,256]{1,0:T(8,128)(2,1)S(1)}, bf16[272,256]{1,0:T(8,128)(2,1)S(1)}, u32[]{:S(2)}, u32[]{:S(2)}) collective-permute-start(bf16[272,256]{1,0:T(8,128)(2,1)S(1)} %shard_map.61.p0_ref), channel_id=1, source_target_pairs={{0,128},{2,130},{4,132},{6,134},{8,136},{10,138},{12,140},{14,142}... | collective-permute-start | bytes 417800 | tf_op jit(solution)/shard_map/ppermute | solution.py:354
  93.1 23.2 %collective-permute-start.6 = (bf16[272,256]{1,0:T(8,128)(2,1)S(1)}, bf16[272,256]{1,0:T(8,128)(2,1)S(1)}, u32[]{:S(2)}, u32[]{:S(2)}) collective-permute-start(bf16[272,256]{1,0:T(8,128)(2,1)S(1)} %shard_map.61.p0_ref), channel_id=1, source_target_pairs={{0,256},{2,258},{4,260},{6,262},{8,264},{10,266},{12,268},{14,270}... | collective-permute-start | bytes 417800 | tf_op jit(solution)/shard_map/ppermute | solution.py:354
  99.2 17.1 %collective-permute-start.7 = (bf16[272,256]{1,0:T(8,128)(2,1)S(1)}, bf16[272,256]{1,0:T(8,128)(2,1)S(1)}, u32[]{:S(2)}, u32[]{:S(2)}) collective-permute-start(bf16[272,256]{1,0:T(8,128)(2,1)S(1)} %shard_map.61.p0_ref), channel_id=1, source_target_pairs={{0,384},{2,386},{4,388},{6,390},{8,392},{10,394},{12,396},{14,398}... | collective-permute-start | bytes 417800 | tf_op jit(solution)/shard_map/ppermute | solution.py:354
  116.9 4.0 %collective-permute-start.8 = (bf16[4,272,256]{2,1,0:T(8,128)(2,1)S(1)}, bf16[4,272,256]{2,1,0:T(8,128)(2,1)S(1)}, u32[]{:S(2)}, u32[]{:S(2)}) collective-permute-start(bf16[4,272,256]{2,1,0:T(8,128)(2,1)S(1)} %shard_map.62.own_ref), channel_id=1, source_target_pairs={{0,1},{1,0},{2,3},{3,2},{4,5},{5,4},{6,7},{7,6},{8,9},{9,8},{10,11... | collective-permute-start | bytes 1671176 | tf_op jit(solution)/shard_map/ppermute | solution.py:334
  132.4 31.2 %copy-start = (s32[16,3]{0,1:T(4,128)S(1)}, s32[16,3]{0,1:T(4,128)}, u32[]{:S(2)}) copy-start(s32[16,3]{0,1:T(4,128)} %param.5) | copy-start | bytes 580
  159.4 6.3 %collective-permute-start.9 = (bf16[16,56,512]{2,1,0:T(8,128)(2,1)S(1)}, bf16[16,56,512]{2,1,0:T(8,128)(2,1)S(1)}, u32[]{:S(2)}, u32[]{:S(2)}) collective-permute-start(bf16[16,56,512]{2,1,0:T(8,128)(2,1)S(1)} %all_to_all.11.own_ref), channel_id=1, source_target_pairs={{0,1},{1,0},{2,3},{3,2},{4,5},{5,4},{6,7},{7,6},{8,9},{9,8},{10,11... | collective-permute-start | bytes 2752520 | tf_op jit(solution)/shard_map/ppermute | solution.py:334

commit v3 on v2

--- a/solution.py
+++ b/solution.py
@@ -22,6 +22,8 @@
 COEF_Q = -4.775
 COEF_T = 2.0315
 
+IDLE = 3
+
 
 F32 = jnp.float32
 BF16 = jnp.bfloat16
@@ -41,36 +43,64 @@
     return lax.dot_general(a, b, (((0,), (0,)), ((), ())), preferred_element_type=F32)
 
 
-def blend_kernel(c_ref, grad_ref, mom_ref, new_ref, keep_ref, send_ref, sum_ref):
+def blend_kernel(
+    c_ref, grad_ref, mom_ref, new_ref, keep_ref, send_ref, sum_ref, gbuf, mbuf, gsem, msem, nsem
+):
     first = c_ref[0] == 0
-    grad = grad_ref[0]
-    new = MU * mom_ref[0] + grad
-    new_ref[0] = new
-    blended = (grad + MU * new).astype(BF16)
-    left, right = blended[:, :HALF], blended[:, HALF:]
-    keep_ref[0] = jnp.where(first, left, right)
-    send_ref[0] = jnp.where(first, right, left)
-    rounded = blended.astype(F32)
-    total = jnp.sum(jnp.sum(rounded * rounded, axis=0, keepdims=True), axis=1, keepdims=True)
-    sum_ref[0] = jnp.broadcast_to(total, (8, 128))
+    count = gbuf.shape[0]
+    loads = [
+        (
+            pltpu.make_async_copy(grad_ref.at[i], gbuf.at[i], gsem.at[i]),
+            pltpu.make_async_copy(mom_ref.at[i], mbuf.at[i], msem.at[i]),
+        )
+        for i in range(count)
+    ]
+    for pair in loads:
+        for copy in pair:
+            copy.start()
+    stores = []
+    for i, pair in enumerate(loads):
+        for copy in pair:
+            copy.wait()
+        grad = gbuf[i]
+        new = MU * mbuf[i] + grad
+        mbuf[i] = new
+        store = pltpu.make_async_copy(mbuf.at[i], new_ref.at[i], nsem.at[i])
+        store.start()
+        stores.append(store)
+        blended = (grad + MU * new).astype(BF16)
+        left, right = blended[:, :HALF], blended[:, HALF:]
+        keep_ref[i] = jnp.where(first, left, right)
+        send_ref[i] = jnp.where(first, right, left)
+        rounded = blended.astype(F32)
+        total = jnp.sum(jnp.sum(rounded * rounded, axis=0, keepdims=True), axis=1, keepdims=True)
+        sum_ref[i] = jnp.broadcast_to(total, (8, 128))
+    for store in stores:
+        store.wait()
 
 
 def blend(ctl, grad, momentum):
     count = grad.shape[0]
-    full = pl.BlockSpec((1, SHARD, FF), lambda i: (i, 0, 0))
-    half = pl.BlockSpec((1, SHARD, HALF), lambda i: (i, 0, 0))
+    whole = (count, SHARD, FF)
+    hbm = pl.BlockSpec(memory_space=pltpu.HBM)
     return pl.pallas_call(
         blend_kernel,
-        grid=(count,),
-        in_specs=[SMEM, full, full],
-        out_specs=[full, half, half, pl.BlockSpec((1, 8, 128), lambda i: (i, 0, 0))],
+        in_specs=[SMEM, hbm, hbm],
+        out_specs=[hbm, VMEM, VMEM, VMEM],
         out_shape=[
-            jax.ShapeDtypeStruct((count, SHARD, FF), F32),
+            jax.ShapeDtypeStruct(whole, F32),
             jax.ShapeDtypeStruct((count, SHARD, HALF), BF16),
             jax.ShapeDtypeStruct((count, SHARD, HALF), BF16),
             jax.ShapeDtypeStruct((count, 8, 128), F32),
         ],
-        compiler_params=params(16),
+        scratch_shapes=[
+            pltpu.VMEM(whole, F32),
+            pltpu.VMEM(whole, F32),
+            pltpu.SemaphoreType.DMA((count,)),
+            pltpu.SemaphoreType.DMA((count,)),
+            pltpu.SemaphoreType.DMA((count,)),
+        ],
+        compiler_params=params(24),
     )(ctl, grad, momentum)
 
 
@@ -88,7 +118,7 @@
         for k in range(3):
             i = (q % 2) * 3 + k
             out_ref[k * 4 + q] = jnp.where(c == q // 2, keep_ref[i], recv_ref[i])
-        out_ref[12 + q] = note
+        out_ref[IDLE * 4 + q] = note
 
 
 def pack(ctl, keep, recv, sums):
@@ -158,10 +188,10 @@
     total = p0_ref[...].astype(F32) + p1_ref[...].astype(F32)
     total = total + (p2_ref[...].astype(F32) + p3_ref[...].astype(F32))
     out_ref[...] = total.astype(BF16)
-    y = c_ref[3]
+    row, _ = index_grid((16, BLK))
     note = p0_ref[:16].astype(F32)
     for j, ref in enumerate((p1_ref, p2_ref, p3_ref)):
-        note = jnp.where(y == j + 1, ref[:16].astype(F32), note)
+        note = jnp.where(row >= 4 * j + 4, ref[:16].astype(F32), note)
     out_ref[:16] = jnp.where(c_ref[1] == 1, note, total[:16]).astype(BF16)
 
 
@@ -171,21 +201,6 @@
         in_specs=[SMEM] + [VMEM] * 4,
         out_specs=VMEM,
         out_shape=jax.ShapeDtypeStruct((CHUNK, BLK), BF16),
-        compiler_params=params(16),
-    )(ctl, *parts)
-
-
-def collect_kernel(c_ref, p0_ref, p1_ref, p2_ref, p3_ref, out_ref):
-    for j, ref in enumerate((p0_ref, p1_ref, p2_ref, p3_ref)):
-        out_ref[lax.rem(c_ref[2] + 4 - j, 4)] = ref[...]
-
-
-def collect(ctl, parts):
-    return pl.pallas_call(
-        collect_kernel,
-        in_specs=[SMEM] + [VMEM] * 4,
-        out_specs=VMEM,
-        out_shape=jax.ShapeDtypeStruct((4, CHUNK, BLK), BF16),
         compiler_params=params(16),
     )(ctl, *parts)
 
@@ -261,12 +276,11 @@
     for s in blocks:
         wb[s] = (w32[s] + dot(mb[s], nb[...])).astype(BF16)
 
-    notes = []
-    for j in range(4):
-        at = lax.rem(c_ref[2] + 4 - j, 4)
-        both = own_ref[at, :16].astype(F32) + oth_ref[at, :16].astype(F32)
-        notes.append((both[:, :128] + both[:, 128:])[0:1])
-    note = jnp.concatenate(notes, axis=1)
+    norms = own_ref[0, :16].astype(F32) + oth_ref[0, :16].astype(F32)
+    for i in range(1, 4):
+        norms = norms + (own_ref[i, :16].astype(F32) + oth_ref[i, :16].astype(F32))
+    norms = norms[:, :128] + norms[:, 128:]
+    note = jnp.concatenate([norms[4 * j : 4 * j + 1] for j in range(4)], axis=1)
     high = note.astype(BF16).astype(F32)
     spot = lax.broadcasted_iota(jnp.int32, (ROWS, HALF), 0)
     note = jnp.where(spot < 16, high, note - high)
@@ -307,35 +321,30 @@
 
 
 def join_kernel(c_ref, own_ref, oth_ref, out_ref):
-    first = c_ref[0] == 0
-    own, oth = own_ref[0], oth_ref[0]
-    out_ref[0, :, :HALF] = jnp.where(first, own, oth)
-    out_ref[0, :, HALF:] = jnp.where(first, oth, own)
-
-
-def join(core, own, oth):
-    def slot(i, c):
-        return ((i % 3) * 4 + 2 * c[0] + i // 3, 0, 0)
-
+    c = c_ref[0]
+    for i in range(6):
+        slot = (i % 3) * 4 + 2 * c + i // 3
+        own, oth = own_ref[slot], oth_ref[slot]
+        out_ref[i, :, :HALF] = jnp.where(c == 0, own, oth)
+        out_ref[i, :, HALF:] = jnp.where(c == 0, oth, own)
+
+
+def join(ctl, own, oth):
     return pl.pallas_call(
         join_kernel,
-        grid_spec=pltpu.PrefetchScalarGridSpec(
-            num_scalar_prefetch=1,
-            grid=(6,),
-            in_specs=[pl.BlockSpec((1, SHARD, HALF), slot)] * 2,
-            out_specs=pl.BlockSpec((1, SHARD, FF), lambda i, c: (i, 0, 0)),
-        ),
+        in_specs=[SMEM, VMEM, VMEM],
+        out_specs=VMEM,
         out_shape=jax.ShapeDtypeStruct((6, SHARD, FF), BF16),
         compiler_params=params(16),
-    )(core, own, oth)
+    )(ctl, own, oth)
 
 
 def swap(value):
     return lax.ppermute(value, "c", [(0, 1), (1, 0)])
 
 
-def owner_rms(notes, owners):
-    norms = jnp.sum(notes[:, 0].astype(F32) + notes[:, 16].astype(F32), axis=0)
+def owner_rms(note, owners):
+    norms = note[0].astype(F32) + note[16].astype(F32)
     norms = norms.reshape(4, 128)[:, :12].reshape(4, 4, 3)
     x = lax.axis_index("x")
     table = owners.reshape(4, 4, 3)
@@ -344,20 +353,18 @@
     return jnp.sqrt(jnp.sum(jnp.where(turned == me, norms, 0.0)) / (D * FF)).reshape(1)
 
 
-def between(value, shift, idle_pair):
+def between(value, shift):
     pairs = []
     for a, b, y, x in itertools.product(range(4), repeat=4):
-        target = ((a + shift) % 4, b, y, x) if b < 3 else idle_pair(a, y, x)
-        if target is not None:
-            index = [((h * 4 + i) * 4 + j) * 4 + k for h, i, j, k in ((a, b, y, x), target)]
-            pairs.append(tuple(index))
+        target = (a, b, y, (x + shift) % 4) if b == IDLE else ((a + shift) % 4, b, y, x)
+        pairs.append(tuple(((h * 4 + i) * 4 + j) * 4 + k for h, i, j, k in ((a, b, y, x), target)))
     return lax.ppermute(value, ("a", "b", "y", "x"), pairs)
 
 
 def shards(grad, momentum, owners):
     shape = grad.shape
-    index = [lax.axis_index("c"), lax.axis_index("b") == 3, lax.axis_index("a"), lax.axis_index("y")]
-    ctl = jnp.stack([i.astype(jnp.int32) for i in index])
+    core, a, b = (lax.axis_index(name).astype(jnp.int32) for name in ("c", "a", "b"))
+    ctl = jnp.stack([core, (b == IDLE).astype(jnp.int32), a])
     flat = (6, SHARD, FF)
     grad = pltpu.with_memory_space_constraint(grad.reshape(flat), pltpu.HBM)
     momentum = pltpu.with_memory_space_constraint(momentum.reshape(flat), pltpu.HBM)
@@ -366,20 +373,13 @@
     own = lax.all_to_all(packed, ("b", "y"), 0, 0, tiled=True)
     oth = swap(own)
     partial = partial_gram(ctl, own, oth)
-    parts = [partial[0]]
-    for j in (1, 2, 3):
-        far = lambda a, y, x, j=j: ((a + j) % 4, 3, y, x) if y == j else None
-        parts.append(between(partial[j], j, far))
-    mine = sum_parts(ctl, parts)
-    parts = [mine]
-    for j in (1, 2, 3):
-        parts.append(between(mine, j, lambda a, y, x, j=j: (a, 3, y, (x + j) % 4)))
-    own_gram = collect(ctl, parts)
+    parts = [partial[0]] + [between(partial[j], j) for j in (1, 2, 3)]
+    own_gram = lax.all_gather(sum_parts(ctl, parts), "a", axis=0)
     oth_gram = swap(own_gram)
     finished = polynomial(ctl, own_gram, oth_gram, own, oth)
     back = lax.all_to_all(finished, ("b", "y"), 0, 0, tiled=True)
     update = join(ctl, back, swap(back))
-    owned_rms = owner_rms(back[12:], owners)
+    owned_rms = owner_rms(back[IDLE * 4], owners)
     return (momentum_new.reshape(shape), update.reshape(shape), owned_rms)
 
 

time: 170 us -> 163 us (0.959)
  blocking collectives: 52.7 us -> 81 us
  starting transfers between devices: 61.1 us -> 42.8 us
  waiting for transfers between devices: 29.1 us -> 14.9 us
  Pallas kernels: 22.3 us -> 19.1 us
    all_gather x0 -> x1, blocking collectives: none -> 28.4 us  [shards(): own_gram = lax.all_gather(sum_parts(ctl, parts), 'a', axis=0)]
    ppermute x6 -> x3, starting transfers between devices: 41.5 us -> 21.9 us  [between(): return lax.ppermute(value, ('a', 'b', 'y', 'x'), pairs)]
    ppermute x6 -> x3, waiting for transfers between devices: 24.4 us -> 10.2 us  [between(): return lax.ppermute(value, ('a', 'b', 'y', 'x'), pairs)]
    pallas_call x3 -> x2, Pallas kernels: 8.11 us -> 4.83 us  [the longest x1 3.39 us: blend(): pl.pallas_call(blend_kernel, in_specs=[SMEM, hbm, hbm], out_specs=[hbm, V...]
  transfers between devices with their start and end apart: 10 -> 7, of which waited for: 6 -> 5; matrix products, arithmetic and copies ran while one was open for 1% -> 1% of each run, Pallas kernels for 0% -> 0%
where the time goes in v3:
time: 163 us; the launch traced here: 162 us
  blocking collectives  81 us (50%)
  starting transfers between devices  42.8 us (26%)
  Pallas kernels  19.1 us (12%)
  waiting for transfers between devices  14.9 us (9%)
  between operations  2.67 us (2%)
    all_gather x1, blocking collectives, shards(): own_gram = lax.all_gather(sum_parts(ctl, parts), 'a', axis=0)  28.4 us
    all_to_all x1, blocking collectives, shards(): back = lax.all_to_all(finished, ('b', 'y'), 0, 0, tiled=True)  27 us
    all_to_all x1, blocking collectives, shards(): own = lax.all_to_all(packed, ('b', 'y'), 0, 0, tiled=True)  25.7 us
    ppermute x3, starting transfers between devices, between(): return lax.ppermute(value, ('a', 'b', 'y', 'x'), pairs)  21.9 us
    ppermute x4, starting transfers between devices, swap(): return lax.ppermute(value, 'c', [(0, 1), (1, 0)])  20.8 us
    pallas_call x1, Pallas kernels, polynomial(): pl.pallas_call(polynomial_kernel, in_specs=[SMEM, VMEM, VMEM, VMEM, VMEM]...  11.5 us
    ppermute x3, waiting for transfers between devices, between(): return lax.ppermute(value, ('a', 'b', 'y', 'x'), pairs)  10.2 us
    ppermute x4, waiting for transfers between devices, swap(): return lax.ppermute(value, 'c', [(0, 1), (1, 0)])  4.72 us
  transfers between devices with their start and end apart: 7, of which 5 were waited for; matrix products, arithmetic and copies ran while one was open for 1% of the time, Pallas kernels for 0%

profile of v3, /device:TPU:1, one launch (start us, length us, event | category | flops | bytes accessed | tf_op | source)
XLA Modules:
  0.0 162.0 jit_solution(6478102088005510681)
XLA Ops:
  0.6 0.1 pad_add_fusion.c_ref
  0.7 3.4 %shard_map.58 = (f32[6,56,1024]{2,1,0:T(8,128)}, bf16[6,56,512]{2,1,0:T(8,128)(2,1)S(1)}, bf16[6,56,512]{2,1,0:T(8,128)(2,1)S(1)}, f32[6,8,128]{2,1,0:T(8,128)S(1)}) custom-call(s32[3]{0:T(128)S(1)} %pad_add_fusion.c_ref, f32[6,56,1024]{2,1,0:T(8,128)} %bitcast.14, f32[6,56,1024]{2,1,0:T(8,128)} %bitcast.15), custom_call_target="tpu_custom_call" | custom-call | tf_op jit(solution)/shard_map/pallas_call | solution.py:86
  4.1 8.8 %collective-permute-start = (bf16[6,56,512]{2,1,0:T(8,128)(2,1)S(1)}, bf16[6,56,512]{2,1,0:T(8,128)(2,1)S(1)}, u32[]{:S(2)}, u32[]{:S(2)}) collective-permute-start(bf16[6,56,512]{2,1,0:T(8,128)(2,1)S(1)} %get-tuple-element.13), channel_id=1, source_target_pairs={{0,1},{1,0},{2,3},{3,2},{4,5},{5,4},{6,7},{7,6},{8,9},{9,8},{10,11... | collective-permute-start | bytes 1032200 | tf_op jit(solution)/shard_map/ppermute | solution.py:343
  12.9 1.3 collective-permute-done.recv_ref
  14.2 0.6 shard_map.59
  14.8 25.7 %all_to_all.10.own_ref.xo_ref = bf16[16,56,512]{2,1,0:T(8,128)(2,1)S(1)} all-to-all(bf16[16,56,512]{2,1,0:T(8,128)(2,1)S(1)} %shard_map.59), channel_id=1, replica_groups=mesh['a'=4,'b'=4,'y'=4,'x'=4,'c'=2] {'b','y'}, dimensions={0} | all-to-all | bytes 1835008 | tf_op jit(solution)/shard_map/all_to_all | solution.py:373
  40.5 4.1 %collective-permute-start.1 = (bf16[16,56,512]{2,1,0:T(8,128)(2,1)S(1)}, bf16[16,56,512]{2,1,0:T(8,128)(2,1)S(1)}, u32[]{:S(2)}, u32[]{:S(2)}) collective-permute-start(bf16[16,56,512]{2,1,0:T(8,128)(2,1)S(1)} %all_to_all.10.own_ref.xo_ref), channel_id=1, source_target_pairs={{0,1},{1,0},{2,3},{3,2},{4,5},{5,4},{6,7},{7,6},{8,9},{9,8},{10,11... | collective-permute-start | bytes 2752520 | tf_op jit(solution)/shard_map/ppermute | solution.py:343
  44.6 2.1 %collective-permute-done.1.oth_ref.xt_ref = bf16[16,56,512]{2,1,0:T(8,128)(2,1)S(1)} collective-permute-done((bf16[16,56,512]{2,1,0:T(8,128)(2,1)S(1)}, bf16[16,56,512]{2,1,0:T(8,128)(2,1)S(1)}, u32[]{:S(2)}, u32[]{:S(2)}) %collective-permute-start.1) | collective-permute-done | bytes 917536 | tf_op jit(solution)/shard_map/ppermute | solution.py:343
  46.6 1.5 shard_map.60
  48.2 8.8 %collective-permute-start.2 = (bf16[272,256]{1,0:T(8,128)(2,1)S(1)}, bf16[272,256]{1,0:T(8,128)(2,1)S(1)}, u32[]{:S(2)}, u32[]{:S(2)}) collective-permute-start(bf16[272,256]{1,0:T(8,128)(2,1)S(1)} %get-tuple-element.16), channel_id=1, source_target_pairs={{0,128},{2,130},{4,132},{6,134},{8,136},{10,138},{12,140},{14,142}... | collective-permute-start | bytes 417800 | tf_op jit(solution)/shard_map/ppermute | solution.py:361
  57.0 7.9 %collective-permute-start.3 = (bf16[272,256]{1,0:T(8,128)(2,1)S(1)}, bf16[272,256]{1,0:T(8,128)(2,1)S(1)}, u32[]{:S(2)}, u32[]{:S(2)}) collective-permute-start(bf16[272,256]{1,0:T(8,128)(2,1)S(1)} %get-tuple-element.17), channel_id=1, source_target_pairs={{0,256},{2,258},{4,260},{6,262},{8,264},{10,266},{12,268},{14,270}... | collective-permute-start | bytes 417800 | tf_op jit(solution)/shard_map/ppermute | solution.py:361
  64.9 5.2 %collective-permute-start.4 = (bf16[272,256]{1,0:T(8,128)(2,1)S(1)}, bf16[272,256]{1,0:T(8,128)(2,1)S(1)}, u32[]{:S(2)}, u32[]{:S(2)}) collective-permute-start(bf16[272,256]{1,0:T(8,128)(2,1)S(1)} %get-tuple-element.18), channel_id=1, source_target_pairs={{0,384},{2,386},{4,388},{6,390},{8,392},{10,394},{12,396},{14,398}... | collective-permute-start | bytes 417800 | tf_op jit(solution)/shard_map/ppermute | solution.py:361
  70.1 0.0 collective-permute-done.2.p1_ref
  70.1 7.5 %collective-permute-done.3.p2_ref = bf16[272,256]{1,0:T(8,128)(2,1)S(1)} collective-permute-done((bf16[272,256]{1,0:T(8,128)(2,1)S(1)}, bf16[272,256]{1,0:T(8,128)(2,1)S(1)}, u32[]{:S(2)}, u32[]{:S(2)}) %collective-permute-start.3) | collective-permute-done | bytes 139296 | tf_op jit(solution)/shard_map/ppermute | solution.py:361
  77.6 2.7 %collective-permute-done.4.p3_ref = bf16[272,256]{1,0:T(8,128)(2,1)S(1)} collective-permute-done((bf16[272,256]{1,0:T(8,128)(2,1)S(1)}, bf16[272,256]{1,0:T(8,128)(2,1)S(1)}, u32[]{:S(2)}, u32[]{:S(2)}) %collective-permute-start.4) | collective-permute-done | bytes 139296 | tf_op jit(solution)/shard_map/ppermute | solution.py:361
  80.3 0.6 shard_map.61
  81.0 28.4 %all-gather = bf16[1088,256]{1,0:T(8,128)(2,1)S(1)} all-gather(bf16[272,256]{1,0:T(8,128)(2,1)S(1)} %shard_map.61), channel_id=2, replica_groups=mesh['a'=4,'b'=4,'y'=4,'x'=4,'c'=2] {'a'}, dimensions={0}, use_global_device_ids=true | all-gather | bytes 696320 | tf_op jit(solution)/shard_map/all_gather | solution.py:377
  109.3 3.9 %collective-permute-start.5 = (bf16[4,272,256]{2,1,0:T(8,128)(2,1)S(1)}, bf16[4,272,256]{2,1,0:T(8,128)(2,1)S(1)}, u32[]{:S(2)}, u32[]{:S(2)}) collective-permute-start(bf16[4,272,256]{2,1,0:T(8,128)(2,1)S(1)} %bitcast.12), channel_id=1, source_target_pairs={{0,1},{1,0},{2,3},{3,2},{4,5},{5,4},{6,7},{7,6},{8,9},{9,8},{10,11... | collective-permute-start | bytes 1671176 | tf_op jit(solution)/shard_map/ppermute | solution.py:343
  113.2 1.4 collective-permute-done.5.oth_ref
  114.6 11.5 %shard_map.62 = bf16[16,56,512]{2,1,0:T(8,128)(2,1)S(1)} custom-call(s32[3]{0:T(128)S(1)} %pad_add_fusion.c_ref, bf16[4,272,256]{2,1,0:T(8,128)(2,1)S(1)} %bitcast.13, bf16[4,272,256]{2,1,0:T(8,128)(2,1)S(1)} %collective-permute-done.5.oth_ref, bf16[16,56,512]{2,1,0:T(8,128)(2,1)S(1)} %all_to_all.10.own_ref.xo_ref, ...), custom_call_target="tpu_custom_call" | custom-call | tf_op jit(solution)/shard_map/pallas_call | solution.py:300
  126.1 0.0 copy-start
  126.1 27.0 %all_to_all.11.own_ref = bf16[16,56,512]{2,1,0:T(8,128)(2,1)S(1)} all-to-all(bf16[16,56,512]{2,1,0:T(8,128)(2,1)S(1)} %shard_map.62), channel_id=1, replica_groups=mesh['a'=4,'b'=4,'y'=4,'x'=4,'c'=2] {'b','y'}, dimensions={0} | all-to-all | bytes 1835008 | tf_op jit(solution)/shard_map/all_to_all | solution.py:380
  153.1 4.1 %collective-permute-start.6 = (bf16[16,56,512]{2,1,0:T(8,128)(2,1)S(1)}, bf16[16,56,512]{2,1,0:T(8,128)(2,1)S(1)}, u32[]{:S(2)}, u32[]{:S(2)}) collective-permute-start(bf16[16,56,512]{2,1,0:T(8,128)(2,1)S(1)} %all_to_all.11.own_ref), channel_id=1, source_target_pairs={{0,1},{1,0},{2,3},{3,2},{4,5},{5,4},{6,7},{7,6},{8,9},{9,8},{10,11... | collective-permute-start | bytes 2752520 | tf_op jit(solution)/shard_map/ppermute | solution.py:343
  157.3 0.0 copy-done
  157.3 0.1 reshape.43
  157.4 0.1 copy.13
  157.5 0.1 stack.38
  157.6 0.1 copy.12
  157.7 0.1 stack.37
  157.7 0.1 copy.11
  157.8 0.1 stack.36
  157.9 0.1 copy.10
  158.0 0.1 stack.35
  158.1 0.6 select_reduce_fusion
  159.4 0.0 collective-permute-done.6.oth_ref
  159.4 1.4 shard_map.63
  (2 shorter events, 0.0 us)
Async XLA Ops:
  4.1 10.1 %collective-permute-start = (bf16[6,56,512]{2,1,0:T(8,128)(2,1)S(1)}, bf16[6,56,512]{2,1,0:T(8,128)(2,1)S(1)}, u32[]{:S(2)}, u32[]{:S(2)}) collective-permute-start(bf16[6,56,512]{2,1,0:T(8,128)(2,1)S(1)} %get-tuple-element.13), channel_id=1, source_target_pairs={{0,1},{1,0},{2,3},{3,2},{4,5},{5,4},{6,7},{7,6},{8,9},{9,8},{10,11... | collective-permute-start | bytes 1032200 | tf_op jit(solution)/shard_map/ppermute | solution.py:343
  40.5 6.2 %collective-permute-start.1 = (bf16[16,56,512]{2,1,0:T(8,128)(2,1)S(1)}, bf16[16,56,512]{2,1,0:T(8,128)(2,1)S(1)}, u32[]{:S(2)}, u32[]{:S(2)}) collective-permute-start(bf16[16,56,512]{2,1,0:T(8,128)(2,1)S(1)} %all_to_all.10.own_ref.xo_ref), channel_id=1, source_target_pairs={{0,1},{1,0},{2,3},{3,2},{4,5},{5,4},{6,7},{7,6},{8,9},{9,8},{10,11... | collective-permute-start | bytes 2752520 | tf_op jit(solution)/shard_map/ppermute | solution.py:343
  48.2 22.0 %collective-permute-start.2 = (bf16[272,256]{1,0:T(8,128)(2,1)S(1)}, bf16[272,256]{1,0:T(8,128)(2,1)S(1)}, u32[]{:S(2)}, u32[]{:S(2)}) collective-permute-start(bf16[272,256]{1,0:T(8,128)(2,1)S(1)} %get-tuple-element.16), channel_id=1, source_target_pairs={{0,128},{2,130},{4,132},{6,134},{8,136},{10,138},{12,140},{14,142}... | collective-permute-start | bytes 417800 | tf_op jit(solution)/shard_map/ppermute | solution.py:361
  57.0 20.7 %collective-permute-start.3 = (bf16[272,256]{1,0:T(8,128)(2,1)S(1)}, bf16[272,256]{1,0:T(8,128)(2,1)S(1)}, u32[]{:S(2)}, u32[]{:S(2)}) collective-permute-start(bf16[272,256]{1,0:T(8,128)(2,1)S(1)} %get-tuple-element.17), channel_id=1, source_target_pairs={{0,256},{2,258},{4,260},{6,262},{8,264},{10,266},{12,268},{14,270}... | collective-permute-start | bytes 417800 | tf_op jit(solution)/shard_map/ppermute | solution.py:361
  64.9 15.4 %collective-permute-start.4 = (bf16[272,256]{1,0:T(8,128)(2,1)S(1)}, bf16[272,256]{1,0:T(8,128)(2,1)S(1)}, u32[]{:S(2)}, u32[]{:S(2)}) collective-permute-start(bf16[272,256]{1,0:T(8,128)(2,1)S(1)} %get-tuple-element.18), channel_id=1, source_target_pairs={{0,384},{2,386},{4,388},{6,390},{8,392},{10,394},{12,396},{14,398}... | collective-permute-start | bytes 417800 | tf_op jit(solution)/shard_map/ppermute | solution.py:361
  109.3 5.3 %collective-permute-start.5 = (bf16[4,272,256]{2,1,0:T(8,128)(2,1)S(1)}, bf16[4,272,256]{2,1,0:T(8,128)(2,1)S(1)}, u32[]{:S(2)}, u32[]{:S(2)}) collective-permute-start(bf16[4,272,256]{2,1,0:T(8,128)(2,1)S(1)} %bitcast.12), channel_id=1, source_target_pairs={{0,1},{1,0},{2,3},{3,2},{4,5},{5,4},{6,7},{7,6},{8,9},{9,8},{10,11... | collective-permute-start | bytes 1671176 | tf_op jit(solution)/shard_map/ppermute | solution.py:343
  126.1 31.2 %copy-start = (s32[16,3]{0,1:T(4,128)S(1)}, s32[16,3]{0,1:T(4,128)}, u32[]{:S(2)}) copy-start(s32[16,3]{0,1:T(4,128)} %param.5) | copy-start | bytes 580
  153.1 6.3 %collective-permute-start.6 = (bf16[16,56,512]{2,1,0:T(8,128)(2,1)S(1)}, bf16[16,56,512]{2,1,0:T(8,128)(2,1)S(1)}, u32[]{:S(2)}, u32[]{:S(2)}) collective-permute-start(bf16[16,56,512]{2,1,0:T(8,128)(2,1)S(1)} %all_to_all.11.own_ref), channel_id=1, source_target_pairs={{0,1},{1,0},{2,3},{3,2},{4,5},{5,4},{6,7},{7,6},{8,9},{9,8},{10,11... | collective-permute-start | bytes 2752520 | tf_op jit(solution)/shard_map/ppermute | solution.py:343

commit v4 on v3

--- a/solution.py
+++ b/solution.py
@@ -43,65 +43,82 @@
     return lax.dot_general(a, b, (((0,), (0,)), ((), ())), preferred_element_type=F32)
 
 
-def blend_kernel(
-    c_ref, grad_ref, mom_ref, new_ref, keep_ref, send_ref, sum_ref, gbuf, mbuf, gsem, msem, nsem
-):
-    first = c_ref[0] == 0
-    count = gbuf.shape[0]
-    loads = [
-        (
-            pltpu.make_async_copy(grad_ref.at[i], gbuf.at[i], gsem.at[i]),
-            pltpu.make_async_copy(mom_ref.at[i], mbuf.at[i], msem.at[i]),
+def loads(grad_ref, mom_ref, gbuf, mbuf, gsem, msem):
+    copies = []
+    for i in range(gbuf.shape[0]):
+        copies.append(
+            (
+                pltpu.make_async_copy(grad_ref.at[i], gbuf.at[i], gsem.at[i]),
+                pltpu.make_async_copy(mom_ref.at[i], mbuf.at[i], msem.at[i]),
+            )
         )
-        for i in range(count)
-    ]
-    for pair in loads:
+    for pair in copies:
         for copy in pair:
             copy.start()
-    stores = []
-    for i, pair in enumerate(loads):
+    return copies
+
+
+def blend_kernel(c_ref, grad_ref, mom_ref, keep_ref, send_ref, sum_ref, gbuf, mbuf, gsem, msem):
+    first = c_ref[0] == 0
+    for i, pair in enumerate(loads(grad_ref, mom_ref, gbuf, mbuf, gsem, msem)):
         for copy in pair:
             copy.wait()
         grad = gbuf[i]
-        new = MU * mbuf[i] + grad
-        mbuf[i] = new
-        store = pltpu.make_async_copy(mbuf.at[i], new_ref.at[i], nsem.at[i])
-        store.start()
-        stores.append(store)
-        blended = (grad + MU * new).astype(BF16)
+        blended = (grad + MU * (MU * mbuf[i] + grad)).astype(BF16)
         left, right = blended[:, :HALF], blended[:, HALF:]
         keep_ref[i] = jnp.where(first, left, right)
         send_ref[i] = jnp.where(first, right, left)
         rounded = blended.astype(F32)
         total = jnp.sum(jnp.sum(rounded * rounded, axis=0, keepdims=True), axis=1, keepdims=True)
         sum_ref[i] = jnp.broadcast_to(total, (8, 128))
+
+
+def momentum_kernel(grad_ref, mom_ref, after_ref, new_ref, gbuf, mbuf, gsem, msem, nsem):
+    stores = []
+    for i, pair in enumerate(loads(grad_ref, mom_ref, gbuf, mbuf, gsem, msem)):
+        for copy in pair:
+            copy.wait()
+        mbuf[i] = MU * mbuf[i] + gbuf[i]
+        store = pltpu.make_async_copy(mbuf.at[i], new_ref.at[i], nsem.at[i])
+        store.start()
+        stores.append(store)
     for store in stores:
         store.wait()
 
 
+def buffers(count, groups):
+    whole = pltpu.VMEM((count, SHARD, FF), F32)
+    return [whole, whole] + [pltpu.SemaphoreType.DMA((count,))] * groups
+
+
+HBM = pl.BlockSpec(memory_space=pltpu.HBM)
+
+
 def blend(ctl, grad, momentum):
     count = grad.shape[0]
-    whole = (count, SHARD, FF)
-    hbm = pl.BlockSpec(memory_space=pltpu.HBM)
     return pl.pallas_call(
         blend_kernel,
-        in_specs=[SMEM, hbm, hbm],
-        out_specs=[hbm, VMEM, VMEM, VMEM],
+        in_specs=[SMEM, HBM, HBM],
+        out_specs=[VMEM, VMEM, VMEM],
         out_shape=[
-            jax.ShapeDtypeStruct(whole, F32),
             jax.ShapeDtypeStruct((count, SHARD, HALF), BF16),
             jax.ShapeDtypeStruct((count, SHARD, HALF), BF16),
             jax.ShapeDtypeStruct((count, 8, 128), F32),
         ],
-        scratch_shapes=[
-            pltpu.VMEM(whole, F32),
-            pltpu.VMEM(whole, F32),
-            pltpu.SemaphoreType.DMA((count,)),
-            pltpu.SemaphoreType.DMA((count,)),
-            pltpu.SemaphoreType.DMA((count,)),
-        ],
+        scratch_shapes=buffers(count, 2),
         compiler_params=params(24),
     )(ctl, grad, momentum)
+
+
+def new_momentum(grad, momentum, after):
+    return pl.pallas_call(
+        momentum_kernel,
+        in_specs=[HBM, HBM, pl.BlockSpec(memory_space=pl.ANY)],
+        out_specs=HBM,
+        out_shape=jax.ShapeDtypeStruct(grad.shape, F32),
+        scratch_shapes=buffers(grad.shape[0], 3),
+        compiler_params=params(24),
+    )(grad, momentum, after)
 
 
 def pack_kernel(c_ref, keep_ref, recv_ref, sum_ref, out_ref):
@@ -257,20 +274,28 @@
     put_pair(1, 3, jnp.where(first, p3, r3t), jnp.where(first, p3t, r3))
 
     blocks = [slice(i * BLK, (i + 1) * BLK) for i in range(4)]
+    def mirrored(i, value, half, full):
+        for j in range(i, 4):
+            block = value[:, (j - i) * BLK : (j - i + 1) * BLK]
+            pairs = ((i, j, block),) if i == j else ((i, j, block), (j, i, block.T))
+            for r, c, piece in pairs:
+                full[blocks[r], blocks[c]] = piece.astype(BF16)
+                if half is not None and c < 2:
+                    half[blocks[r], blocks[c]] = piece
+
+    for i, s in enumerate(blocks):
+        right = slice(i * BLK, FF)
+        mirrored(i, COEF_Q * a32[s, right] + COEF_T * dot(ab[s], ab[:, right]), m32, mb)
+    for i, s in enumerate(blocks):
+        right = slice(i * BLK, FF)
+        prod = COEF_P * a32[s, right] + dot(ab[s], mb[:, right])
+        c32[s, right] = prod
+        mirrored(i, prod, None, cb)
+    for i, s in enumerate(blocks):
+        right = slice(i * BLK, FF)
+        mirrored(i, COEF_P * c32[s, right] + dot(cb[s], mb[:, right]), a32, gb)
     for s in blocks:
-        poly = COEF_Q * a32[s] + COEF_T * dot(ab[s], ab[...])
-        m32[s] = poly[:, :HALF]
-        mb[s] = poly.astype(BF16)
-    for s in blocks:
-        prod = COEF_P * a32[s] + dot(ab[s], mb[...])
-        c32[s] = prod
-        cb[s] = prod.astype(BF16)
-    for s in blocks:
-        gram = COEF_P * c32[s] + dot(cb[s], mb[...])
-        c32[s] = gram
-        gb[s] = gram.astype(BF16)
-    for s in blocks:
-        poly = COEF_Q * c32[s, :HALF] + COEF_T * dot(gb[s], gb[:, :HALF])
+        poly = COEF_Q * a32[s, :HALF] + COEF_T * dot(gb[s], gb[:, :HALF])
         nb[s] = poly.astype(BF16)
         w32[s] = COEF_P * (poly + m32[s])
     for s in blocks:
@@ -368,12 +393,14 @@
     flat = (6, SHARD, FF)
     grad = pltpu.with_memory_space_constraint(grad.reshape(flat), pltpu.HBM)
     momentum = pltpu.with_memory_space_constraint(momentum.reshape(flat), pltpu.HBM)
-    momentum_new, keep, send, sums = blend(ctl, grad, momentum)
+    keep, send, sums = blend(ctl, grad, momentum)
     packed = pack(ctl, keep, swap(send), sums)
     own = lax.all_to_all(packed, ("b", "y"), 0, 0, tiled=True)
     oth = swap(own)
     partial = partial_gram(ctl, own, oth)
     parts = [partial[0]] + [between(partial[j], j) for j in (1, 2, 3)]
+    momentum_new = new_momentum(grad, momentum, partial[0])
+    *parts, momentum_new = lax.optimization_barrier((*parts, momentum_new))
     own_gram = lax.all_gather(sum_parts(ctl, parts), "a", axis=0)
     oth_gram = swap(own_gram)
     finished = polynomial(ctl, own_gram, oth_gram, own, oth)

time: 163 us -> 159 us (0.975)
  waiting for transfers between devices: 14.9 us -> 12.4 us
    pallas_call x1, Pallas kernels: 11.5 us -> 8.71 us  [polynomial(): pl.pallas_call(polynomial_kernel, in_specs=[SMEM, VMEM, VMEM, VMEM, VMEM]...]
    ppermute x3, waiting for transfers between devices: 10.2 us -> 7.51 us  [between(): return lax.ppermute(value, ('a', 'b', 'y', 'x'), pairs)]
    pallas_call x1 -> x2, Pallas kernels: 3.39 us -> 5.48 us  [the longest x1 2.77 us: blend(): pl.pallas_call(blend_kernel, in_specs=[SMEM, HBM, HBM], out_specs=[VMEM,...]
  transfers between devices with their start and end apart: 7 -> 7, of which waited for: 5 -> 5; matrix products, arithmetic and copies ran while one was open for 1% -> 1% of each run, Pallas kernels for 0% -> 2%
where the time goes in v4:
time: 159 us
  blocking collectives  81.3 us (51%)
  starting transfers between devices  42.5 us (27%)
  Pallas kernels  18.4 us (12%)
  waiting for transfers between devices  12.4 us (8%)
  between operations  2.67 us (2%)
    all_gather x1, blocking collectives, shards(): own_gram = lax.all_gather(sum_parts(ctl, parts), 'a', axis=0)  28.3 us
    all_to_all x1, blocking collectives, shards(): back = lax.all_to_all(finished, ('b', 'y'), 0, 0, tiled=True)  27.3 us
    all_to_all x1, blocking collectives, shards(): own = lax.all_to_all(packed, ('b', 'y'), 0, 0, tiled=True)  25.7 us
    ppermute x3, starting transfers between devices, between(): return lax.ppermute(value, ('a', 'b', 'y', 'x'), pairs)  21.9 us
    ppermute x4, starting transfers between devices, swap(): return lax.ppermute(value, 'c', [(0, 1), (1, 0)])  20.5 us
    pallas_call x1, Pallas kernels, polynomial(): pl.pallas_call(polynomial_kernel, in_specs=[SMEM, VMEM, VMEM, VMEM, VMEM]...  8.71 us
    ppermute x3, waiting for transfers between devices, between(): return lax.ppermute(value, ('a', 'b', 'y', 'x'), pairs)  7.51 us
    ppermute x4, waiting for transfers between devices, swap(): return lax.ppermute(value, 'c', [(0, 1), (1, 0)])  4.9 us
  transfers between devices with their start and end apart: 7, of which 5 were waited for; matrix products, arithmetic and copies ran while one was open for 1% of the time, Pallas kernels for 2%

profile of v4, /device:TPU:1, one launch (start us, length us, event | category | flops | bytes accessed | tf_op | source)
XLA Modules:
  0.0 158.7 jit_solution(3657500893087061617)
XLA Ops:
  0.6 0.1 pad_add_fusion.c_ref
  0.7 2.8 %shard_map.58 = (bf16[6,56,512]{2,1,0:T(8,128)(2,1)S(1)}, bf16[6,56,512]{2,1,0:T(8,128)(2,1)S(1)}, f32[6,8,128]{2,1,0:T(8,128)S(1)}) custom-call(s32[3]{0:T(128)S(1)} %pad_add_fusion.c_ref, f32[6,56,1024]{2,1,0:T(8,128)} %bitcast.14, f32[6,56,1024]{2,1,0:T(8,128)} %bitcast.16), custom_call_target="tpu_custom_call" | custom-call | tf_op jit(solution)/shard_map/pallas_call | solution.py:99
  3.5 8.8 %collective-permute-start = (bf16[6,56,512]{2,1,0:T(8,128)(2,1)S(1)}, bf16[6,56,512]{2,1,0:T(8,128)(2,1)S(1)}, u32[]{:S(2)}, u32[]{:S(2)}) collective-permute-start(bf16[6,56,512]{2,1,0:T(8,128)(2,1)S(1)} %get-tuple-element.16), channel_id=1, source_target_pairs={{0,1},{1,0},{2,3},{3,2},{4,5},{5,4},{6,7},{7,6},{8,9},{9,8},{10,11... | collective-permute-start | bytes 1032200 | tf_op jit(solution)/shard_map/ppermute | solution.py:368
  12.3 1.3 collective-permute-done.recv_ref
  13.6 0.6 shard_map.59
  14.2 25.7 %all_to_all.10.own_ref.xo_ref = bf16[16,56,512]{2,1,0:T(8,128)(2,1)S(1)} all-to-all(bf16[16,56,512]{2,1,0:T(8,128)(2,1)S(1)} %shard_map.59), channel_id=1, replica_groups=mesh['a'=4,'b'=4,'y'=4,'x'=4,'c'=2] {'b','y'}, dimensions={0} | all-to-all | bytes 1835008 | tf_op jit(solution)/shard_map/all_to_all | solution.py:398
  39.8 4.1 %collective-permute-start.1 = (bf16[16,56,512]{2,1,0:T(8,128)(2,1)S(1)}, bf16[16,56,512]{2,1,0:T(8,128)(2,1)S(1)}, u32[]{:S(2)}, u32[]{:S(2)}) collective-permute-start(bf16[16,56,512]{2,1,0:T(8,128)(2,1)S(1)} %all_to_all.10.own_ref.xo_ref), channel_id=1, source_target_pairs={{0,1},{1,0},{2,3},{3,2},{4,5},{5,4},{6,7},{7,6},{8,9},{9,8},{10,11... | collective-permute-start | bytes 2752520 | tf_op jit(solution)/shard_map/ppermute | solution.py:368
  43.9 2.1 %collective-permute-done.1.oth_ref.xt_ref = bf16[16,56,512]{2,1,0:T(8,128)(2,1)S(1)} collective-permute-done((bf16[16,56,512]{2,1,0:T(8,128)(2,1)S(1)}, bf16[16,56,512]{2,1,0:T(8,128)(2,1)S(1)}, u32[]{:S(2)}, u32[]{:S(2)}) %collective-permute-start.1) | collective-permute-done | bytes 917536 | tf_op jit(solution)/shard_map/ppermute | solution.py:368
  46.0 1.5 shard_map.60
  47.5 8.8 %collective-permute-start.2 = (bf16[272,256]{1,0:T(8,128)(2,1)S(1)}, bf16[272,256]{1,0:T(8,128)(2,1)S(1)}, u32[]{:S(2)}, u32[]{:S(2)}) collective-permute-start(bf16[272,256]{1,0:T(8,128)(2,1)S(1)} %get-tuple-element.19), channel_id=1, source_target_pairs={{0,128},{2,130},{4,132},{6,134},{8,136},{10,138},{12,140},{14,142}... | collective-permute-start | bytes 417800 | tf_op jit(solution)/shard_map/ppermute | solution.py:386
  56.4 7.9 %collective-permute-start.3 = (bf16[272,256]{1,0:T(8,128)(2,1)S(1)}, bf16[272,256]{1,0:T(8,128)(2,1)S(1)}, u32[]{:S(2)}, u32[]{:S(2)}) collective-permute-start(bf16[272,256]{1,0:T(8,128)(2,1)S(1)} %get-tuple-element.20), channel_id=1, source_target_pairs={{0,256},{2,258},{4,260},{6,262},{8,264},{10,266},{12,268},{14,270}... | collective-permute-start | bytes 417800 | tf_op jit(solution)/shard_map/ppermute | solution.py:386
  64.3 5.2 %collective-permute-start.4 = (bf16[272,256]{1,0:T(8,128)(2,1)S(1)}, bf16[272,256]{1,0:T(8,128)(2,1)S(1)}, u32[]{:S(2)}, u32[]{:S(2)}) collective-permute-start(bf16[272,256]{1,0:T(8,128)(2,1)S(1)} %get-tuple-element.21), channel_id=1, source_target_pairs={{0,384},{2,386},{4,388},{6,390},{8,392},{10,394},{12,396},{14,398}... | collective-permute-start | bytes 417800 | tf_op jit(solution)/shard_map/ppermute | solution.py:386
  69.5 2.7 %shard_map.61 = f32[6,56,1024]{2,1,0:T(8,128)} custom-call(f32[6,56,1024]{2,1,0:T(8,128)} %bitcast.15, f32[6,56,1024]{2,1,0:T(8,128)} %bitcast.17, bf16[272,256]{1,0:T(8,128)(2,1)S(1)} %get-tuple-element.23.after_ref.p0_ref), custom_call_target="tpu_custom_call" | custom-call | tf_op jit(solution)/shard_map/pallas_call | solution.py:114
  72.2 0.0 collective-permute-done.2.p1_ref
  72.2 4.8 %collective-permute-done.3.p2_ref = bf16[272,256]{1,0:T(8,128)(2,1)S(1)} collective-permute-done((bf16[272,256]{1,0:T(8,128)(2,1)S(1)}, bf16[272,256]{1,0:T(8,128)(2,1)S(1)}, u32[]{:S(2)}, u32[]{:S(2)}) %collective-permute-start.3) | collective-permute-done | bytes 139296 | tf_op jit(solution)/shard_map/ppermute | solution.py:386
  77.0 2.7 %collective-permute-done.4.p3_ref = bf16[272,256]{1,0:T(8,128)(2,1)S(1)} collective-permute-done((bf16[272,256]{1,0:T(8,128)(2,1)S(1)}, bf16[272,256]{1,0:T(8,128)(2,1)S(1)}, u32[]{:S(2)}, u32[]{:S(2)}) %collective-permute-start.4) | collective-permute-done | bytes 139296 | tf_op jit(solution)/shard_map/ppermute | solution.py:386
  79.7 0.6 shard_map.62
  80.4 28.3 %all-gather = bf16[1088,256]{1,0:T(8,128)(2,1)S(1)} all-gather(bf16[272,256]{1,0:T(8,128)(2,1)S(1)} %shard_map.62), channel_id=2, replica_groups=mesh['a'=4,'b'=4,'y'=4,'x'=4,'c'=2] {'a'}, dimensions={0}, use_global_device_ids=true | all-gather | bytes 696320 | tf_op jit(solution)/shard_map/all_gather | solution.py:404
  108.7 3.5 %collective-permute-start.5 = (bf16[4,272,256]{2,1,0:T(8,128)(2,1)S(1)}, bf16[4,272,256]{2,1,0:T(8,128)(2,1)S(1)}, u32[]{:S(2)}, u32[]{:S(2)}) collective-permute-start(bf16[4,272,256]{2,1,0:T(8,128)(2,1)S(1)} %bitcast.12), channel_id=1, source_target_pairs={{0,1},{1,0},{2,3},{3,2},{4,5},{5,4},{6,7},{7,6},{8,9},{9,8},{10,11... | collective-permute-start | bytes 1671176 | tf_op jit(solution)/shard_map/ppermute | solution.py:368
  112.2 1.6 collective-permute-done.5.oth_ref
  113.8 8.7 %shard_map.63 = bf16[16,56,512]{2,1,0:T(8,128)(2,1)S(1)} custom-call(s32[3]{0:T(128)S(1)} %pad_add_fusion.c_ref, bf16[4,272,256]{2,1,0:T(8,128)(2,1)S(1)} %bitcast.13, bf16[4,272,256]{2,1,0:T(8,128)(2,1)S(1)} %collective-permute-done.5.oth_ref, bf16[16,56,512]{2,1,0:T(8,128)(2,1)S(1)} %all_to_all.10.own_ref.xo_ref, ...), custom_call_target="tpu_custom_call" | custom-call | tf_op jit(solution)/shard_map/pallas_call | solution.py:325
  122.5 0.0 copy-start
  122.5 27.3 %all_to_all.11.own_ref = bf16[16,56,512]{2,1,0:T(8,128)(2,1)S(1)} all-to-all(bf16[16,56,512]{2,1,0:T(8,128)(2,1)S(1)} %shard_map.63), channel_id=1, replica_groups=mesh['a'=4,'b'=4,'y'=4,'x'=4,'c'=2] {'b','y'}, dimensions={0} | all-to-all | bytes 1835008 | tf_op jit(solution)/shard_map/all_to_all | solution.py:407
  149.8 4.1 %collective-permute-start.6 = (bf16[16,56,512]{2,1,0:T(8,128)(2,1)S(1)}, bf16[16,56,512]{2,1,0:T(8,128)(2,1)S(1)}, u32[]{:S(2)}, u32[]{:S(2)}) collective-permute-start(bf16[16,56,512]{2,1,0:T(8,128)(2,1)S(1)} %all_to_all.11.own_ref), channel_id=1, source_target_pairs={{0,1},{1,0},{2,3},{3,2},{4,5},{5,4},{6,7},{7,6},{8,9},{9,8},{10,11... | collective-permute-start | bytes 2752520 | tf_op jit(solution)/shard_map/ppermute | solution.py:368
  154.0 0.0 copy-done
  154.0 0.1 reshape.43
  154.1 0.1 copy.13
  154.2 0.1 stack.38
  154.3 0.1 copy.12
  154.4 0.1 stack.37
  154.4 0.1 copy.11
  154.5 0.1 stack.36
  154.6 0.1 copy.10
  154.7 0.1 stack.35
  154.8 0.6 select_reduce_fusion
  156.1 0.0 collective-permute-done.6.oth_ref
  156.1 1.4 shard_map.64
  (2 shorter events, 0.0 us)
Async XLA Ops:
  3.5 10.1 %collective-permute-start = (bf16[6,56,512]{2,1,0:T(8,128)(2,1)S(1)}, bf16[6,56,512]{2,1,0:T(8,128)(2,1)S(1)}, u32[]{:S(2)}, u32[]{:S(2)}) collective-permute-start(bf16[6,56,512]{2,1,0:T(8,128)(2,1)S(1)} %get-tuple-element.16), channel_id=1, source_target_pairs={{0,1},{1,0},{2,3},{3,2},{4,5},{5,4},{6,7},{7,6},{8,9},{9,8},{10,11... | collective-permute-start | bytes 1032200 | tf_op jit(solution)/shard_map/ppermute | solution.py:368
  39.8 6.2 %collective-permute-start.1 = (bf16[16,56,512]{2,1,0:T(8,128)(2,1)S(1)}, bf16[16,56,512]{2,1,0:T(8,128)(2,1)S(1)}, u32[]{:S(2)}, u32[]{:S(2)}) collective-permute-start(bf16[16,56,512]{2,1,0:T(8,128)(2,1)S(1)} %all_to_all.10.own_ref.xo_ref), channel_id=1, source_target_pairs={{0,1},{1,0},{2,3},{3,2},{4,5},{5,4},{6,7},{7,6},{8,9},{9,8},{10,11... | collective-permute-start | bytes 2752520 | tf_op jit(solution)/shard_map/ppermute | solution.py:368
  47.5 24.7 %collective-permute-start.2 = (bf16[272,256]{1,0:T(8,128)(2,1)S(1)}, bf16[272,256]{1,0:T(8,128)(2,1)S(1)}, u32[]{:S(2)}, u32[]{:S(2)}) collective-permute-start(bf16[272,256]{1,0:T(8,128)(2,1)S(1)} %get-tuple-element.19), channel_id=1, source_target_pairs={{0,128},{2,130},{4,132},{6,134},{8,136},{10,138},{12,140},{14,142}... | collective-permute-start | bytes 417800 | tf_op jit(solution)/shard_map/ppermute | solution.py:386
  56.4 20.7 %collective-permute-start.3 = (bf16[272,256]{1,0:T(8,128)(2,1)S(1)}, bf16[272,256]{1,0:T(8,128)(2,1)S(1)}, u32[]{:S(2)}, u32[]{:S(2)}) collective-permute-start(bf16[272,256]{1,0:T(8,128)(2,1)S(1)} %get-tuple-element.20), channel_id=1, source_target_pairs={{0,256},{2,258},{4,260},{6,262},{8,264},{10,266},{12,268},{14,270}... | collective-permute-start | bytes 417800 | tf_op jit(solution)/shard_map/ppermute | solution.py:386
  64.3 15.4 %collective-permute-start.4 = (bf16[272,256]{1,0:T(8,128)(2,1)S(1)}, bf16[272,256]{1,0:T(8,128)(2,1)S(1)}, u32[]{:S(2)}, u32[]{:S(2)}) collective-permute-start(bf16[272,256]{1,0:T(8,128)(2,1)S(1)} %get-tuple-element.21), channel_id=1, source_target_pairs={{0,384},{2,386},{4,388},{6,390},{8,392},{10,394},{12,396},{14,398}... | collective-permute-start | bytes 417800 | tf_op jit(solution)/shard_map/ppermute | solution.py:386
  108.7 5.1 %collective-permute-start.5 = (bf16[4,272,256]{2,1,0:T(8,128)(2,1)S(1)}, bf16[4,272,256]{2,1,0:T(8,128)(2,1)S(1)}, u32[]{:S(2)}, u32[]{:S(2)}) collective-permute-start(bf16[4,272,256]{2,1,0:T(8,128)(2,1)S(1)} %bitcast.12), channel_id=1, source_target_pairs={{0,1},{1,0},{2,3},{3,2},{4,5},{5,4},{6,7},{7,6},{8,9},{9,8},{10,11... | collective-permute-start | bytes 1671176 | tf_op jit(solution)/shard_map/ppermute | solution.py:368
  122.5 31.5 %copy-start = (s32[16,3]{0,1:T(4,128)S(1)}, s32[16,3]{0,1:T(4,128)}, u32[]{:S(2)}) copy-start(s32[16,3]{0,1:T(4,128)} %param.5) | copy-start | bytes 580
  149.8 6.3 %collective-permute-start.6 = (bf16[16,56,512]{2,1,0:T(8,128)(2,1)S(1)}, bf16[16,56,512]{2,1,0:T(8,128)(2,1)S(1)}, u32[]{:S(2)}, u32[]{:S(2)}) collective-permute-start(bf16[16,56,512]{2,1,0:T(8,128)(2,1)S(1)} %all_to_all.11.own_ref), channel_id=1, source_target_pairs={{0,1},{1,0},{2,3},{3,2},{4,5},{5,4},{6,7},{7,6},{8,9},{9,8},{10,11... | collective-permute-start | bytes 2752520 | tf_op jit(solution)/shard_map/ppermute | solution.py:368

commit v5 on v4

--- a/solution.py
+++ b/solution.py
@@ -205,10 +205,9 @@
     total = p0_ref[...].astype(F32) + p1_ref[...].astype(F32)
     total = total + (p2_ref[...].astype(F32) + p3_ref[...].astype(F32))
     out_ref[...] = total.astype(BF16)
-    row, _ = index_grid((16, BLK))
     note = p0_ref[:16].astype(F32)
     for j, ref in enumerate((p1_ref, p2_ref, p3_ref)):
-        note = jnp.where(row >= 4 * j + 4, ref[:16].astype(F32), note)
+        note = jnp.where(c_ref[3] == j + 1, ref[:16].astype(F32), note)
     out_ref[:16] = jnp.where(c_ref[1] == 1, note, total[:16]).astype(BF16)
 
 
@@ -301,11 +300,8 @@
     for s in blocks:
         wb[s] = (w32[s] + dot(mb[s], nb[...])).astype(BF16)
 
-    norms = own_ref[0, :16].astype(F32) + oth_ref[0, :16].astype(F32)
-    for i in range(1, 4):
-        norms = norms + (own_ref[i, :16].astype(F32) + oth_ref[i, :16].astype(F32))
-    norms = norms[:, :128] + norms[:, 128:]
-    note = jnp.concatenate([norms[4 * j : 4 * j + 1] for j in range(4)], axis=1)
+    notes = [own_ref[i, :16].astype(F32) + oth_ref[i, :16].astype(F32) for i in range(4)]
+    note = jnp.concatenate([(n[:, :128] + n[:, 128:])[0:1] for n in notes], axis=1)
     high = note.astype(BF16).astype(F32)
     spot = lax.broadcasted_iota(jnp.int32, (ROWS, HALF), 0)
     note = jnp.where(spot < 16, high, note - high)
@@ -368,28 +364,33 @@
     return lax.ppermute(value, "c", [(0, 1), (1, 0)])
 
 
-def owner_rms(note, owners):
-    norms = note[0].astype(F32) + note[16].astype(F32)
-    norms = norms.reshape(4, 128)[:, :12].reshape(4, 4, 3)
-    x = lax.axis_index("x")
-    table = owners.reshape(4, 4, 3)
-    turned = jnp.stack([lax.dynamic_index_in_dim(table, (x - j) % 4, 0, False) for j in range(4)])
+def owner_rms(notes, owners):
+    norms = jnp.sum(notes[:, 0].astype(F32) + notes[:, 16].astype(F32), axis=0)
+    norms = norms.reshape(4, 128)[:, :12].reshape(owners.shape)
     me = (lax.axis_index("a") * 4 + lax.axis_index("b")) * 4 + lax.axis_index("y")
-    return jnp.sqrt(jnp.sum(jnp.where(turned == me, norms, 0.0)) / (D * FF)).reshape(1)
+    return jnp.sqrt(jnp.sum(jnp.where(owners == me, norms, 0.0)) / (D * FF)).reshape(1)
 
 
 def between(value, shift):
     pairs = []
     for a, b, y, x in itertools.product(range(4), repeat=4):
-        target = (a, b, y, (x + shift) % 4) if b == IDLE else ((a + shift) % 4, b, y, x)
-        pairs.append(tuple(((h * 4 + i) * 4 + j) * 4 + k for h, i, j, k in ((a, b, y, x), target)))
+        if b != IDLE or y == shift:
+            ends = ((a, b, y, x), ((a + shift) % 4, b, y, x))
+            pairs.append(tuple(((h * 4 + i) * 4 + j) * 4 + k for h, i, j, k in ends))
     return lax.ppermute(value, ("a", "b", "y", "x"), pairs)
+
+
+def gather(value):
+    groups = [[(a * 4 + b) * 4 + x for a in range(4)] for b in range(IDLE) for x in range(4)]
+    groups += [[(a * 4 + IDLE) * 4 + x for x in range(4)] for a in range(4)]
+    return lax.all_gather(value, ("a", "b", "x"), axis=0, axis_index_groups=groups)
 
 
 def shards(grad, momentum, owners):
     shape = grad.shape
     core, a, b = (lax.axis_index(name).astype(jnp.int32) for name in ("c", "a", "b"))
-    ctl = jnp.stack([core, (b == IDLE).astype(jnp.int32), a])
+    y = lax.axis_index("y").astype(jnp.int32)
+    ctl = jnp.stack([core, (b == IDLE).astype(jnp.int32), a, y])
     flat = (6, SHARD, FF)
     grad = pltpu.with_memory_space_constraint(grad.reshape(flat), pltpu.HBM)
     momentum = pltpu.with_memory_space_constraint(momentum.reshape(flat), pltpu.HBM)
@@ -401,12 +402,12 @@
     parts = [partial[0]] + [between(partial[j], j) for j in (1, 2, 3)]
     momentum_new = new_momentum(grad, momentum, partial[0])
     *parts, momentum_new = lax.optimization_barrier((*parts, momentum_new))
-    own_gram = lax.all_gather(sum_parts(ctl, parts), "a", axis=0)
+    own_gram = gather(sum_parts(ctl, parts))
     oth_gram = swap(own_gram)
     finished = polynomial(ctl, own_gram, oth_gram, own, oth)
     back = lax.all_to_all(finished, ("b", "y"), 0, 0, tiled=True)
     update = join(ctl, back, swap(back))
-    owned_rms = owner_rms(back[IDLE * 4], owners)
+    owned_rms = owner_rms(back[IDLE * 4 :], owners)
     return (momentum_new.reshape(shape), update.reshape(shape), owned_rms)
 
 

time: 159 us -> 157 us (0.987)
  blocking collectives: 81.3 us -> 79.7 us
    all_gather x1, blocking collectives: 28.3 us -> 25.3 us  [gather(): lax.all_gather(value, ('a', 'b', 'x'), axis=0, axis_index_groups=groups)]
  transfers between devices with their start and end apart: 7 -> 7, of which waited for: 5 -> 6; matrix products, arithmetic and copies ran while one was open for 1% -> 1% of each run, Pallas kernels for 2% -> 2%
where the time goes in v5:
time: 157 us
  blocking collectives  79.7 us (51%)
  starting transfers between devices  42.6 us (27%)
  Pallas kernels  18.4 us (12%)
  waiting for transfers between devices  12.8 us (8%)
  between operations  2.59 us (2%)
    all_to_all x1, blocking collectives, shards(): back = lax.all_to_all(finished, ('b', 'y'), 0, 0, tiled=True)  28.7 us
    all_to_all x1, blocking collectives, shards(): own = lax.all_to_all(packed, ('b', 'y'), 0, 0, tiled=True)  25.7 us
    all_gather x1, blocking collectives, gather(): lax.all_gather(value, ('a', 'b', 'x'), axis=0, axis_index_groups=groups)  25.3 us
    ppermute x3, starting transfers between devices, between(): return lax.ppermute(value, ('a', 'b', 'y', 'x'), pairs)  21.9 us
    ppermute x4, starting transfers between devices, swap(): return lax.ppermute(value, 'c', [(0, 1), (1, 0)])  20.6 us
    pallas_call x1, Pallas kernels, polynomial(): pl.pallas_call(polynomial_kernel, in_specs=[SMEM, VMEM, VMEM, VMEM, VMEM]...  8.7 us
    ppermute x3, waiting for transfers between devices, between(): return lax.ppermute(value, ('a', 'b', 'y', 'x'), pairs)  7.37 us
    ppermute x4, waiting for transfers between devices, swap(): return lax.ppermute(value, 'c', [(0, 1), (1, 0)])  5.47 us
  transfers between devices with their start and end apart: 7, of which 6 were waited for; matrix products, arithmetic and copies ran while one was open for 1% of the time, Pallas kernels for 2%

profile of v5, /device:TPU:1, one launch (start us, length us, event | category | flops | bytes accessed | tf_op | source)
XLA Modules:
  0.0 156.9 jit_solution(17555437955371482410)
XLA Ops:
  0.6 0.1 pad_add_fusion.c_ref
  0.7 2.8 %shard_map.58 = (bf16[6,56,512]{2,1,0:T(8,128)(2,1)S(1)}, bf16[6,56,512]{2,1,0:T(8,128)(2,1)S(1)}, f32[6,8,128]{2,1,0:T(8,128)S(1)}) custom-call(s32[4]{0:T(128)S(1)} %pad_add_fusion.c_ref, f32[6,56,1024]{2,1,0:T(8,128)} %bitcast.14, f32[6,56,1024]{2,1,0:T(8,128)} %bitcast.16), custom_call_target="tpu_custom_call" | custom-call | tf_op jit(solution)/shard_map/pallas_call | solution.py:99
  3.5 8.8 %collective-permute-start = (bf16[6,56,512]{2,1,0:T(8,128)(2,1)S(1)}, bf16[6,56,512]{2,1,0:T(8,128)(2,1)S(1)}, u32[]{:S(2)}, u32[]{:S(2)}) collective-permute-start(bf16[6,56,512]{2,1,0:T(8,128)(2,1)S(1)} %get-tuple-element.16), channel_id=1, source_target_pairs={{0,1},{1,0},{2,3},{3,2},{4,5},{5,4},{6,7},{7,6},{8,9},{9,8},{10,11... | collective-permute-start | bytes 1032200 | tf_op jit(solution)/shard_map/ppermute | solution.py:364
  12.3 1.3 collective-permute-done.recv_ref
  13.6 0.6 shard_map.59
  14.2 25.7 %all_to_all.10.own_ref.xo_ref = bf16[16,56,512]{2,1,0:T(8,128)(2,1)S(1)} all-to-all(bf16[16,56,512]{2,1,0:T(8,128)(2,1)S(1)} %shard_map.59), channel_id=1, replica_groups=mesh['a'=4,'b'=4,'y'=4,'x'=4,'c'=2] {'b','y'}, dimensions={0} | all-to-all | bytes 1835008 | tf_op jit(solution)/shard_map/all_to_all | solution.py:399
  39.8 4.1 %collective-permute-start.1 = (bf16[16,56,512]{2,1,0:T(8,128)(2,1)S(1)}, bf16[16,56,512]{2,1,0:T(8,128)(2,1)S(1)}, u32[]{:S(2)}, u32[]{:S(2)}) collective-permute-start(bf16[16,56,512]{2,1,0:T(8,128)(2,1)S(1)} %all_to_all.10.own_ref.xo_ref), channel_id=1, source_target_pairs={{0,1},{1,0},{2,3},{3,2},{4,5},{5,4},{6,7},{7,6},{8,9},{9,8},{10,11... | collective-permute-start | bytes 2752520 | tf_op jit(solution)/shard_map/ppermute | solution.py:364
  43.9 2.1 %collective-permute-done.1.oth_ref.xt_ref = bf16[16,56,512]{2,1,0:T(8,128)(2,1)S(1)} collective-permute-done((bf16[16,56,512]{2,1,0:T(8,128)(2,1)S(1)}, bf16[16,56,512]{2,1,0:T(8,128)(2,1)S(1)}, u32[]{:S(2)}, u32[]{:S(2)}) %collective-permute-start.1) | collective-permute-done | bytes 917536 | tf_op jit(solution)/shard_map/ppermute | solution.py:364
  46.0 1.5 shard_map.60
  47.5 8.8 %collective-permute-start.2 = (bf16[272,256]{1,0:T(8,128)(2,1)S(1)}, bf16[272,256]{1,0:T(8,128)(2,1)S(1)}, u32[]{:S(2)}, u32[]{:S(2)}) collective-permute-start(bf16[272,256]{1,0:T(8,128)(2,1)S(1)} %get-tuple-element.19), channel_id=1, source_target_pairs={{0,128},{2,130},{4,132},{6,134},{8,136},{10,138},{12,140},{14,142}... | collective-permute-start | bytes 417800 | tf_op jit(solution)/shard_map/ppermute | solution.py:380
  56.4 7.9 %collective-permute-start.3 = (bf16[272,256]{1,0:T(8,128)(2,1)S(1)}, bf16[272,256]{1,0:T(8,128)(2,1)S(1)}, u32[]{:S(2)}, u32[]{:S(2)}) collective-permute-start(bf16[272,256]{1,0:T(8,128)(2,1)S(1)} %get-tuple-element.20), channel_id=1, source_target_pairs={{0,256},{2,258},{4,260},{6,262},{8,264},{10,266},{12,268},{14,270}... | collective-permute-start | bytes 417800 | tf_op jit(solution)/shard_map/ppermute | solution.py:380
  64.3 5.2 %collective-permute-start.4 = (bf16[272,256]{1,0:T(8,128)(2,1)S(1)}, bf16[272,256]{1,0:T(8,128)(2,1)S(1)}, u32[]{:S(2)}, u32[]{:S(2)}) collective-permute-start(bf16[272,256]{1,0:T(8,128)(2,1)S(1)} %get-tuple-element.21), channel_id=1, source_target_pairs={{0,384},{2,386},{4,388},{6,390},{8,392},{10,394},{12,396},{14,398}... | collective-permute-start | bytes 417800 | tf_op jit(solution)/shard_map/ppermute | solution.py:380
  69.5 2.7 %shard_map.61 = f32[6,56,1024]{2,1,0:T(8,128)} custom-call(f32[6,56,1024]{2,1,0:T(8,128)} %bitcast.15, f32[6,56,1024]{2,1,0:T(8,128)} %bitcast.17, bf16[272,256]{1,0:T(8,128)(2,1)S(1)} %get-tuple-element.23.after_ref.p0_ref), custom_call_target="tpu_custom_call" | custom-call | tf_op jit(solution)/shard_map/pallas_call | solution.py:114
  72.2 0.0 collective-permute-done.2.p1_ref
  72.2 4.8 %collective-permute-done.3.p2_ref = bf16[272,256]{1,0:T(8,128)(2,1)S(1)} collective-permute-done((bf16[272,256]{1,0:T(8,128)(2,1)S(1)}, bf16[272,256]{1,0:T(8,128)(2,1)S(1)}, u32[]{:S(2)}, u32[]{:S(2)}) %collective-permute-start.3) | collective-permute-done | bytes 139296 | tf_op jit(solution)/shard_map/ppermute | solution.py:380
  77.0 2.6 %collective-permute-done.4.p3_ref = bf16[272,256]{1,0:T(8,128)(2,1)S(1)} collective-permute-done((bf16[272,256]{1,0:T(8,128)(2,1)S(1)}, bf16[272,256]{1,0:T(8,128)(2,1)S(1)}, u32[]{:S(2)}, u32[]{:S(2)}) %collective-permute-start.4) | collective-permute-done | bytes 139296 | tf_op jit(solution)/shard_map/ppermute | solution.py:380
  79.6 0.6 shard_map.62
  80.2 25.3 %all-gather = bf16[1088,256]{1,0:T(8,128)(2,1)S(1)} all-gather(bf16[272,256]{1,0:T(8,128)(2,1)S(1)} %shard_map.62), channel_id=2, replica_groups={{0,128,256,384},{2,130,258,386},{4,132,260,388},{6,134,262,390},{32,160..., dimensions={0}, use_global_device_ids=true | all-gather | bytes 696320 | tf_op jit(solution)/shard_map/all_gather | solution.py:386
  105.5 3.7 %collective-permute-start.5 = (bf16[4,272,256]{2,1,0:T(8,128)(2,1)S(1)}, bf16[4,272,256]{2,1,0:T(8,128)(2,1)S(1)}, u32[]{:S(2)}, u32[]{:S(2)}) collective-permute-start(bf16[4,272,256]{2,1,0:T(8,128)(2,1)S(1)} %bitcast.12), channel_id=1, source_target_pairs={{0,1},{1,0},{2,3},{3,2},{4,5},{5,4},{6,7},{7,6},{8,9},{9,8},{10,11... | collective-permute-start | bytes 1671176 | tf_op jit(solution)/shard_map/ppermute | solution.py:364
  109.2 1.6 collective-permute-done.5.oth_ref
  110.7 8.7 %shard_map.63 = bf16[16,56,512]{2,1,0:T(8,128)(2,1)S(1)} custom-call(s32[4]{0:T(128)S(1)} %pad_add_fusion.c_ref, bf16[4,272,256]{2,1,0:T(8,128)(2,1)S(1)} %bitcast.13, bf16[4,272,256]{2,1,0:T(8,128)(2,1)S(1)} %collective-permute-done.5.oth_ref, bf16[16,56,512]{2,1,0:T(8,128)(2,1)S(1)} %all_to_all.10.own_ref.xo_ref, ...), custom_call_target="tpu_custom_call" | custom-call | tf_op jit(solution)/shard_map/pallas_call | solution.py:321
  119.4 0.0 copy-start
  119.5 28.7 %all_to_all.11.own_ref = bf16[16,56,512]{2,1,0:T(8,128)(2,1)S(1)} all-to-all(bf16[16,56,512]{2,1,0:T(8,128)(2,1)S(1)} %shard_map.63), channel_id=1, replica_groups=mesh['a'=4,'b'=4,'y'=4,'x'=4,'c'=2] {'b','y'}, dimensions={0} | all-to-all | bytes 1835008 | tf_op jit(solution)/shard_map/all_to_all | solution.py:408
  148.2 4.1 %collective-permute-start.6 = (bf16[16,56,512]{2,1,0:T(8,128)(2,1)S(1)}, bf16[16,56,512]{2,1,0:T(8,128)(2,1)S(1)}, u32[]{:S(2)}, u32[]{:S(2)}) collective-permute-start(bf16[16,56,512]{2,1,0:T(8,128)(2,1)S(1)} %all_to_all.11.own_ref), channel_id=1, source_target_pairs={{0,1},{1,0},{2,3},{3,2},{4,5},{5,4},{6,7},{7,6},{8,9},{9,8},{10,11... | collective-permute-start | bytes 2752520 | tf_op jit(solution)/shard_map/ppermute | solution.py:364
  152.3 0.0 copy-done
  152.3 0.1 copy.7
  152.4 0.1 reshape.35
  152.5 0.6 select_reduce_fusion
  153.8 0.6 collective-permute-done.6.oth_ref
  154.4 1.4 shard_map.64
  (1 shorter events, 0.0 us)
Async XLA Ops:
  3.5 10.1 %collective-permute-start = (bf16[6,56,512]{2,1,0:T(8,128)(2,1)S(1)}, bf16[6,56,512]{2,1,0:T(8,128)(2,1)S(1)}, u32[]{:S(2)}, u32[]{:S(2)}) collective-permute-start(bf16[6,56,512]{2,1,0:T(8,128)(2,1)S(1)} %get-tuple-element.16), channel_id=1, source_target_pairs={{0,1},{1,0},{2,3},{3,2},{4,5},{5,4},{6,7},{7,6},{8,9},{9,8},{10,11... | collective-permute-start | bytes 1032200 | tf_op jit(solution)/shard_map/ppermute | solution.py:364
  39.8 6.2 %collective-permute-start.1 = (bf16[16,56,512]{2,1,0:T(8,128)(2,1)S(1)}, bf16[16,56,512]{2,1,0:T(8,128)(2,1)S(1)}, u32[]{:S(2)}, u32[]{:S(2)}) collective-permute-start(bf16[16,56,512]{2,1,0:T(8,128)(2,1)S(1)} %all_to_all.10.own_ref.xo_ref), channel_id=1, source_target_pairs={{0,1},{1,0},{2,3},{3,2},{4,5},{5,4},{6,7},{7,6},{8,9},{9,8},{10,11... | collective-permute-start | bytes 2752520 | tf_op jit(solution)/shard_map/ppermute | solution.py:364
  47.5 24.7 %collective-permute-start.2 = (bf16[272,256]{1,0:T(8,128)(2,1)S(1)}, bf16[272,256]{1,0:T(8,128)(2,1)S(1)}, u32[]{:S(2)}, u32[]{:S(2)}) collective-permute-start(bf16[272,256]{1,0:T(8,128)(2,1)S(1)} %get-tuple-element.19), channel_id=1, source_target_pairs={{0,128},{2,130},{4,132},{6,134},{8,136},{10,138},{12,140},{14,142}... | collective-permute-start | bytes 417800 | tf_op jit(solution)/shard_map/ppermute | solution.py:380
  56.4 20.7 %collective-permute-start.3 = (bf16[272,256]{1,0:T(8,128)(2,1)S(1)}, bf16[272,256]{1,0:T(8,128)(2,1)S(1)}, u32[]{:S(2)}, u32[]{:S(2)}) collective-permute-start(bf16[272,256]{1,0:T(8,128)(2,1)S(1)} %get-tuple-element.20), channel_id=1, source_target_pairs={{0,256},{2,258},{4,260},{6,262},{8,264},{10,266},{12,268},{14,270}... | collective-permute-start | bytes 417800 | tf_op jit(solution)/shard_map/ppermute | solution.py:380
  64.3 15.3 %collective-permute-start.4 = (bf16[272,256]{1,0:T(8,128)(2,1)S(1)}, bf16[272,256]{1,0:T(8,128)(2,1)S(1)}, u32[]{:S(2)}, u32[]{:S(2)}) collective-permute-start(bf16[272,256]{1,0:T(8,128)(2,1)S(1)} %get-tuple-element.21), channel_id=1, source_target_pairs={{0,384},{2,386},{4,388},{6,390},{8,392},{10,394},{12,396},{14,398}... | collective-permute-start | bytes 417800 | tf_op jit(solution)/shard_map/ppermute | solution.py:380
  105.5 5.2 %collective-permute-start.5 = (bf16[4,272,256]{2,1,0:T(8,128)(2,1)S(1)}, bf16[4,272,256]{2,1,0:T(8,128)(2,1)S(1)}, u32[]{:S(2)}, u32[]{:S(2)}) collective-permute-start(bf16[4,272,256]{2,1,0:T(8,128)(2,1)S(1)} %bitcast.12), channel_id=1, source_target_pairs={{0,1},{1,0},{2,3},{3,2},{4,5},{5,4},{6,7},{7,6},{8,9},{9,8},{10,11... | collective-permute-start | bytes 1671176 | tf_op jit(solution)/shard_map/ppermute | solution.py:364
  119.4 32.9 %copy-start = (s32[16,3]{0,1:T(4,128)S(1)}, s32[16,3]{0,1:T(4,128)}, u32[]{:S(2)}) copy-start(s32[16,3]{0,1:T(4,128)} %param.5) | copy-start | bytes 580
  148.2 6.2 %collective-permute-start.6 = (bf16[16,56,512]{2,1,0:T(8,128)(2,1)S(1)}, bf16[16,56,512]{2,1,0:T(8,128)(2,1)S(1)}, u32[]{:S(2)}, u32[]{:S(2)}) collective-permute-start(bf16[16,56,512]{2,1,0:T(8,128)(2,1)S(1)} %all_to_all.11.own_ref), channel_id=1, source_target_pairs={{0,1},{1,0},{2,3},{3,2},{4,5},{5,4},{6,7},{7,6},{8,9},{9,8},{10,11... | collective-permute-start | bytes 2752520 | tf_op jit(solution)/shard_map/ppermute | solution.py:364

commit v6 on v5

--- a/solution.py
+++ b/solution.py
@@ -341,11 +341,26 @@
     )(core, own_gram, oth_gram, own, oth)
 
 
+def pick_kernel(c_ref, back_ref, out_ref):
+    for i in range(6):
+        out_ref[i] = back_ref[(i % 3) * 4 + 2 * (1 - c_ref[0]) + i // 3]
+
+
+def pick(ctl, back):
+    return pl.pallas_call(
+        pick_kernel,
+        in_specs=[SMEM, VMEM],
+        out_specs=VMEM,
+        out_shape=jax.ShapeDtypeStruct((6, SHARD, HALF), BF16),
+        compiler_params=params(16),
+    )(ctl, back)
+
+
 def join_kernel(c_ref, own_ref, oth_ref, out_ref):
     c = c_ref[0]
     for i in range(6):
         slot = (i % 3) * 4 + 2 * c + i // 3
-        own, oth = own_ref[slot], oth_ref[slot]
+        own, oth = own_ref[slot], oth_ref[i]
         out_ref[i, :, :HALF] = jnp.where(c == 0, own, oth)
         out_ref[i, :, HALF:] = jnp.where(c == 0, oth, own)
 
@@ -406,7 +421,7 @@
     oth_gram = swap(own_gram)
     finished = polynomial(ctl, own_gram, oth_gram, own, oth)
     back = lax.all_to_all(finished, ("b", "y"), 0, 0, tiled=True)
-    update = join(ctl, back, swap(back))
+    update = join(ctl, back, swap(pick(ctl, back)))
     owned_rms = owner_rms(back[IDLE * 4 :], owners)
     return (momentum_new.reshape(shape), update.reshape(shape), owned_rms)
 

time: 157 us -> 157 us (level)
  transfers between devices with their start and end apart: 7 -> 7, of which waited for: 6 -> 5; matrix products, arithmetic and copies ran while one was open for 1% -> 1% of each run, Pallas kernels for 2% -> 2%
where the time goes in v6:
time: 157 us
  blocking collectives  79.7 us (51%)
  starting transfers between devices  42.6 us (27%)
  Pallas kernels  18.9 us (12%)
  waiting for transfers between devices  12.3 us (8%)
  between operations  2.6 us (2%)
    all_to_all x1, blocking collectives, shards(): back = lax.all_to_all(finished, ('b', 'y'), 0, 0, tiled=True)  28.7 us
    all_to_all x1, blocking collectives, shards(): own = lax.all_to_all(packed, ('b', 'y'), 0, 0, tiled=True)  25.7 us
    all_gather x1, blocking collectives, gather(): lax.all_gather(value, ('a', 'b', 'x'), axis=0, axis_index_groups=groups)  25.3 us
    ppermute x3, starting transfers between devices, between(): return lax.ppermute(value, ('a', 'b', 'y', 'x'), pairs)  21.9 us
    ppermute x4, starting transfers between devices, swap(): return lax.ppermute(value, 'c', [(0, 1), (1, 0)])  20.7 us
    pallas_call x1, Pallas kernels, polynomial(): pl.pallas_call(polynomial_kernel, in_specs=[SMEM, VMEM, VMEM, VMEM, VMEM]...  8.7 us
    ppermute x3, waiting for transfers between devices, between(): return lax.ppermute(value, ('a', 'b', 'y', 'x'), pairs)  7.37 us
    ppermute x4, waiting for transfers between devices, swap(): return lax.ppermute(value, 'c', [(0, 1), (1, 0)])  4.9 us
  transfers between devices with their start and end apart: 7, of which 5 were waited for; matrix products, arithmetic and copies ran while one was open for 1% of the time, Pallas kernels for 2%

profile of v6, /device:TPU:1, one launch (start us, length us, event | category | flops | bytes accessed | tf_op | source)
XLA Modules:
  0.0 157.0 jit_solution(13141675293361030874)
XLA Ops:
  0.6 0.1 pad_add_fusion.c_ref
  0.7 2.8 %shard_map.58 = (bf16[6,56,512]{2,1,0:T(8,128)(2,1)S(1)}, bf16[6,56,512]{2,1,0:T(8,128)(2,1)S(1)}, f32[6,8,128]{2,1,0:T(8,128)S(1)}) custom-call(s32[4]{0:T(128)S(1)} %pad_add_fusion.c_ref, f32[6,56,1024]{2,1,0:T(8,128)} %bitcast.14, f32[6,56,1024]{2,1,0:T(8,128)} %bitcast.16), custom_call_target="tpu_custom_call" | custom-call | tf_op jit(solution)/shard_map/pallas_call | solution.py:99
  3.5 8.8 %collective-permute-start = (bf16[6,56,512]{2,1,0:T(8,128)(2,1)S(1)}, bf16[6,56,512]{2,1,0:T(8,128)(2,1)S(1)}, u32[]{:S(2)}, u32[]{:S(2)}) collective-permute-start(bf16[6,56,512]{2,1,0:T(8,128)(2,1)S(1)} %get-tuple-element.16), channel_id=1, source_target_pairs={{0,1},{1,0},{2,3},{3,2},{4,5},{5,4},{6,7},{7,6},{8,9},{9,8},{10,11... | collective-permute-start | bytes 1032200 | tf_op jit(solution)/shard_map/ppermute | solution.py:379
  12.3 1.3 collective-permute-done.recv_ref
  13.6 0.6 shard_map.59
  14.2 25.7 %all_to_all.10.own_ref.xo_ref = bf16[16,56,512]{2,1,0:T(8,128)(2,1)S(1)} all-to-all(bf16[16,56,512]{2,1,0:T(8,128)(2,1)S(1)} %shard_map.59), channel_id=1, replica_groups=mesh['a'=4,'b'=4,'y'=4,'x'=4,'c'=2] {'b','y'}, dimensions={0} | all-to-all | bytes 1835008 | tf_op jit(solution)/shard_map/all_to_all | solution.py:414
  39.8 4.1 %collective-permute-start.1 = (bf16[16,56,512]{2,1,0:T(8,128)(2,1)S(1)}, bf16[16,56,512]{2,1,0:T(8,128)(2,1)S(1)}, u32[]{:S(2)}, u32[]{:S(2)}) collective-permute-start(bf16[16,56,512]{2,1,0:T(8,128)(2,1)S(1)} %all_to_all.10.own_ref.xo_ref), channel_id=1, source_target_pairs={{0,1},{1,0},{2,3},{3,2},{4,5},{5,4},{6,7},{7,6},{8,9},{9,8},{10,11... | collective-permute-start | bytes 2752520 | tf_op jit(solution)/shard_map/ppermute | solution.py:379
  43.9 2.1 %collective-permute-done.1.oth_ref.xt_ref = bf16[16,56,512]{2,1,0:T(8,128)(2,1)S(1)} collective-permute-done((bf16[16,56,512]{2,1,0:T(8,128)(2,1)S(1)}, bf16[16,56,512]{2,1,0:T(8,128)(2,1)S(1)}, u32[]{:S(2)}, u32[]{:S(2)}) %collective-permute-start.1) | collective-permute-done | bytes 917536 | tf_op jit(solution)/shard_map/ppermute | solution.py:379
  46.0 1.5 shard_map.60
  47.5 8.8 %collective-permute-start.2 = (bf16[272,256]{1,0:T(8,128)(2,1)S(1)}, bf16[272,256]{1,0:T(8,128)(2,1)S(1)}, u32[]{:S(2)}, u32[]{:S(2)}) collective-permute-start(bf16[272,256]{1,0:T(8,128)(2,1)S(1)} %get-tuple-element.19), channel_id=1, source_target_pairs={{0,128},{2,130},{4,132},{6,134},{8,136},{10,138},{12,140},{14,142}... | collective-permute-start | bytes 417800 | tf_op jit(solution)/shard_map/ppermute | solution.py:395
  56.4 7.9 %collective-permute-start.3 = (bf16[272,256]{1,0:T(8,128)(2,1)S(1)}, bf16[272,256]{1,0:T(8,128)(2,1)S(1)}, u32[]{:S(2)}, u32[]{:S(2)}) collective-permute-start(bf16[272,256]{1,0:T(8,128)(2,1)S(1)} %get-tuple-element.20), channel_id=1, source_target_pairs={{0,256},{2,258},{4,260},{6,262},{8,264},{10,266},{12,268},{14,270}... | collective-permute-start | bytes 417800 | tf_op jit(solution)/shard_map/ppermute | solution.py:395
  64.3 5.2 %collective-permute-start.4 = (bf16[272,256]{1,0:T(8,128)(2,1)S(1)}, bf16[272,256]{1,0:T(8,128)(2,1)S(1)}, u32[]{:S(2)}, u32[]{:S(2)}) collective-permute-start(bf16[272,256]{1,0:T(8,128)(2,1)S(1)} %get-tuple-element.21), channel_id=1, source_target_pairs={{0,384},{2,386},{4,388},{6,390},{8,392},{10,394},{12,396},{14,398}... | collective-permute-start | bytes 417800 | tf_op jit(solution)/shard_map/ppermute | solution.py:395
  69.5 2.7 %shard_map.61 = f32[6,56,1024]{2,1,0:T(8,128)} custom-call(f32[6,56,1024]{2,1,0:T(8,128)} %bitcast.15, f32[6,56,1024]{2,1,0:T(8,128)} %bitcast.17, bf16[272,256]{1,0:T(8,128)(2,1)S(1)} %get-tuple-element.23.after_ref.p0_ref), custom_call_target="tpu_custom_call" | custom-call | tf_op jit(solution)/shard_map/pallas_call | solution.py:114
  72.2 0.0 collective-permute-done.2.p1_ref
  72.2 4.8 %collective-permute-done.3.p2_ref = bf16[272,256]{1,0:T(8,128)(2,1)S(1)} collective-permute-done((bf16[272,256]{1,0:T(8,128)(2,1)S(1)}, bf16[272,256]{1,0:T(8,128)(2,1)S(1)}, u32[]{:S(2)}, u32[]{:S(2)}) %collective-permute-start.3) | collective-permute-done | bytes 139296 | tf_op jit(solution)/shard_map/ppermute | solution.py:395
  77.0 2.6 %collective-permute-done.4.p3_ref = bf16[272,256]{1,0:T(8,128)(2,1)S(1)} collective-permute-done((bf16[272,256]{1,0:T(8,128)(2,1)S(1)}, bf16[272,256]{1,0:T(8,128)(2,1)S(1)}, u32[]{:S(2)}, u32[]{:S(2)}) %collective-permute-start.4) | collective-permute-done | bytes 139296 | tf_op jit(solution)/shard_map/ppermute | solution.py:395
  79.6 0.6 shard_map.62
  80.2 25.3 %all-gather = bf16[1088,256]{1,0:T(8,128)(2,1)S(1)} all-gather(bf16[272,256]{1,0:T(8,128)(2,1)S(1)} %shard_map.62), channel_id=2, replica_groups={{0,128,256,384},{2,130,258,386},{4,132,260,388},{6,134,262,390},{32,160..., dimensions={0}, use_global_device_ids=true | all-gather | bytes 696320 | tf_op jit(solution)/shard_map/all_gather | solution.py:401
  105.5 3.7 %collective-permute-start.5 = (bf16[4,272,256]{2,1,0:T(8,128)(2,1)S(1)}, bf16[4,272,256]{2,1,0:T(8,128)(2,1)S(1)}, u32[]{:S(2)}, u32[]{:S(2)}) collective-permute-start(bf16[4,272,256]{2,1,0:T(8,128)(2,1)S(1)} %bitcast.12), channel_id=1, source_target_pairs={{0,1},{1,0},{2,3},{3,2},{4,5},{5,4},{6,7},{7,6},{8,9},{9,8},{10,11... | collective-permute-start | bytes 1671176 | tf_op jit(solution)/shard_map/ppermute | solution.py:379
  109.2 1.6 collective-permute-done.5.oth_ref
  110.7 8.7 %shard_map.63 = bf16[16,56,512]{2,1,0:T(8,128)(2,1)S(1)} custom-call(s32[4]{0:T(128)S(1)} %pad_add_fusion.c_ref, bf16[4,272,256]{2,1,0:T(8,128)(2,1)S(1)} %bitcast.13, bf16[4,272,256]{2,1,0:T(8,128)(2,1)S(1)} %collective-permute-done.5.oth_ref, bf16[16,56,512]{2,1,0:T(8,128)(2,1)S(1)} %all_to_all.10.own_ref.xo_ref, ...), custom_call_target="tpu_custom_call" | custom-call | tf_op jit(solution)/shard_map/pallas_call | solution.py:321
  119.4 0.0 copy-start
  119.5 28.7 %all_to_all.11.back_ref.own_ref = bf16[16,56,512]{2,1,0:T(8,128)(2,1)S(1)} all-to-all(bf16[16,56,512]{2,1,0:T(8,128)(2,1)S(1)} %shard_map.63), channel_id=1, replica_groups=mesh['a'=4,'b'=4,'y'=4,'x'=4,'c'=2] {'b','y'}, dimensions={0} | all-to-all | bytes 1835008 | tf_op jit(solution)/shard_map/all_to_all | solution.py:423
  148.2 0.6 shard_map.64
  148.8 4.1 %collective-permute-start.6 = (bf16[6,56,512]{2,1,0:T(8,128)(2,1)S(1)}, bf16[6,56,512]{2,1,0:T(8,128)(2,1)S(1)}, u32[]{:S(2)}, u32[]{:S(2)}) collective-permute-start(bf16[6,56,512]{2,1,0:T(8,128)(2,1)S(1)} %shard_map.64), channel_id=1, source_target_pairs={{0,1},{1,0},{2,3},{3,2},{4,5},{5,4},{6,7},{7,6},{8,9},{9,8},{10,11... | collective-permute-start | bytes 1032200 | tf_op jit(solution)/shard_map/ppermute | solution.py:379
  152.9 0.0 copy-done
  152.9 0.1 copy.7
  153.0 0.1 reshape.35
  153.1 0.6 select_reduce_fusion
  154.4 0.0 collective-permute-done.6.oth_ref
  154.4 1.4 shard_map.65
  (1 shorter events, 0.0 us)
Async XLA Ops:
  3.5 10.1 %collective-permute-start = (bf16[6,56,512]{2,1,0:T(8,128)(2,1)S(1)}, bf16[6,56,512]{2,1,0:T(8,128)(2,1)S(1)}, u32[]{:S(2)}, u32[]{:S(2)}) collective-permute-start(bf16[6,56,512]{2,1,0:T(8,128)(2,1)S(1)} %get-tuple-element.16), channel_id=1, source_target_pairs={{0,1},{1,0},{2,3},{3,2},{4,5},{5,4},{6,7},{7,6},{8,9},{9,8},{10,11... | collective-permute-start | bytes 1032200 | tf_op jit(solution)/shard_map/ppermute | solution.py:379
  39.8 6.2 %collective-permute-start.1 = (bf16[16,56,512]{2,1,0:T(8,128)(2,1)S(1)}, bf16[16,56,512]{2,1,0:T(8,128)(2,1)S(1)}, u32[]{:S(2)}, u32[]{:S(2)}) collective-permute-start(bf16[16,56,512]{2,1,0:T(8,128)(2,1)S(1)} %all_to_all.10.own_ref.xo_ref), channel_id=1, source_target_pairs={{0,1},{1,0},{2,3},{3,2},{4,5},{5,4},{6,7},{7,6},{8,9},{9,8},{10,11... | collective-permute-start | bytes 2752520 | tf_op jit(solution)/shard_map/ppermute | solution.py:379
  47.5 24.7 %collective-permute-start.2 = (bf16[272,256]{1,0:T(8,128)(2,1)S(1)}, bf16[272,256]{1,0:T(8,128)(2,1)S(1)}, u32[]{:S(2)}, u32[]{:S(2)}) collective-permute-start(bf16[272,256]{1,0:T(8,128)(2,1)S(1)} %get-tuple-element.19), channel_id=1, source_target_pairs={{0,128},{2,130},{4,132},{6,134},{8,136},{10,138},{12,140},{14,142}... | collective-permute-start | bytes 417800 | tf_op jit(solution)/shard_map/ppermute | solution.py:395
  56.4 20.7 %collective-permute-start.3 = (bf16[272,256]{1,0:T(8,128)(2,1)S(1)}, bf16[272,256]{1,0:T(8,128)(2,1)S(1)}, u32[]{:S(2)}, u32[]{:S(2)}) collective-permute-start(bf16[272,256]{1,0:T(8,128)(2,1)S(1)} %get-tuple-element.20), channel_id=1, source_target_pairs={{0,256},{2,258},{4,260},{6,262},{8,264},{10,266},{12,268},{14,270}... | collective-permute-start | bytes 417800 | tf_op jit(solution)/shard_map/ppermute | solution.py:395
  64.3 15.3 %collective-permute-start.4 = (bf16[272,256]{1,0:T(8,128)(2,1)S(1)}, bf16[272,256]{1,0:T(8,128)(2,1)S(1)}, u32[]{:S(2)}, u32[]{:S(2)}) collective-permute-start(bf16[272,256]{1,0:T(8,128)(2,1)S(1)} %get-tuple-element.21), channel_id=1, source_target_pairs={{0,384},{2,386},{4,388},{6,390},{8,392},{10,394},{12,396},{14,398}... | collective-permute-start | bytes 417800 | tf_op jit(solution)/shard_map/ppermute | solution.py:395
  105.5 5.2 %collective-permute-start.5 = (bf16[4,272,256]{2,1,0:T(8,128)(2,1)S(1)}, bf16[4,272,256]{2,1,0:T(8,128)(2,1)S(1)}, u32[]{:S(2)}, u32[]{:S(2)}) collective-permute-start(bf16[4,272,256]{2,1,0:T(8,128)(2,1)S(1)} %bitcast.12), channel_id=1, source_target_pairs={{0,1},{1,0},{2,3},{3,2},{4,5},{5,4},{6,7},{7,6},{8,9},{9,8},{10,11... | collective-permute-start | bytes 1671176 | tf_op jit(solution)/shard_map/ppermute | solution.py:379
  119.4 33.4 %copy-start = (s32[16,3]{0,1:T(4,128)S(1)}, s32[16,3]{0,1:T(4,128)}, u32[]{:S(2)}) copy-start(s32[16,3]{0,1:T(4,128)} %param.5) | copy-start | bytes 580
  148.8 5.6 %collective-permute-start.6 = (bf16[6,56,512]{2,1,0:T(8,128)(2,1)S(1)}, bf16[6,56,512]{2,1,0:T(8,128)(2,1)S(1)}, u32[]{:S(2)}, u32[]{:S(2)}) collective-permute-start(bf16[6,56,512]{2,1,0:T(8,128)(2,1)S(1)} %shard_map.64), channel_id=1, source_target_pairs={{0,1},{1,0},{2,3},{3,2},{4,5},{5,4},{6,7},{7,6},{8,9},{9,8},{10,11... | collective-permute-start | bytes 1032200 | tf_op jit(solution)/shard_map/ppermute | solution.py:379
